TPU v7x, 256 devices: a whole 4x4x8 slice. The times are simulated.
256 devices in a mesh: ctx: 32 (over z_lo, x, y), tp: 8 (over z_hi, core).
Axes of the slice: x: 4, y: 4, z: 8 (z_hi: 4, z_lo: 2; z = z_hi * 2 + z_lo), core: 2. Of those that a mesh axis runs over, the one named last changes fastest.
Arguments:
- out_grad: bfloat16 [8192, 4096], P('ctx', 'tp'), may hold values from -6 to 6
- gate_act: bfloat16 [8192, 4096], P('ctx', 'tp'), may hold values from -6 to 6
- key_act: bfloat16 [8192, 4096], P('ctx', 'tp'), may hold values from -6 to 6
- value_act: bfloat16 [8192, 4096], P('ctx', 'tp'), may hold values from -6 to 6
- filter_taps: float32 [8192, 4096], P('ctx', 'tp'), may hold values from -6 to 6
- out_weight: bfloat16 [4096, 4096], P('tp'), may hold values from -0.09375 to 0.09375
Outputs:
- grad_gate: bfloat16 [8192, 4096], P('ctx', 'tp')
- grad_key: bfloat16 [8192, 4096], P('ctx', 'tp')
- grad_value: bfloat16 [8192, 4096], P('ctx', 'tp')
- grad_taps: float32 [8192, 4096], P('ctx', 'tp')
All inputs are finite; a program needn't handle non-finite values.
Results may differ from a plain program's by a relative error of at most 0.012.
Values may be sent and summed in bfloat16 or wider, within the bound.
No kernel may reach another device: no remote copies, remote signals or barrier semaphores. Data moves between devices by JAX's collectives and lax.ppermute only.
A program may use at most 128 MiB of HBM per device.

v0:
```python
import math

import jax
import jax.numpy as jnp
from jax import lax
from jax.sharding import PartitionSpec as P


def angles(numerator, denominator):
    radians = 2.0 * math.pi / denominator * (numerator % denominator).astype(jnp.float32)
    return (jnp.cos(radians), jnp.sin(radians))


def contract(form, table, data):
    return jnp.einsum(form, table, data, precision=lax.Precision.HIGHEST)


def products(spectra):
    inner_re, impulse_re, grad_re = (spectra[0][0], spectra[0][1], spectra[0][2])
    inner_im, impulse_im, grad_im = (spectra[1][0], spectra[1][1], spectra[1][2])
    conv_re = impulse_re * inner_re - impulse_im * inner_im
    conv_im = impulse_re * inner_im + impulse_im * inner_re
    back_re = impulse_re * grad_re + impulse_im * grad_im
    back_im = impulse_re * grad_im - impulse_im * grad_re
    taps_re = inner_re * grad_re + inner_im * grad_im
    taps_im = inner_re * grad_im - inner_im * grad_re
    return jnp.stack(
        [jnp.stack([conv_re, back_re, taps_re]), jnp.stack([conv_im, back_im, taps_im])]
    )


def token_path(signals, part_count, position, seq_length):
    row_count = signals.shape[1]
    row_block = row_count // part_count
    spread = lax.all_to_all(signals[:, None], "ctx", split_axis=2, concat_axis=1, tiled=True)
    part_ids = jnp.arange(part_count, dtype=jnp.int32)
    row_ids = position * row_block + jnp.arange(row_block, dtype=jnp.int32)
    time_ids = part_ids[:, None] * row_count + row_ids[None, :]
    half_cos, half_sin = angles(time_ids, 2 * seq_length)
    half_cos = half_cos[None, :, :, None]
    half_sin = half_sin[None, :, :, None]
    real_part = jnp.stack([spread, spread * half_cos], 1)
    imag_part = jnp.stack([jnp.zeros_like(spread), -spread * half_sin], 1)
    part_cos, part_sin = angles(part_ids[:, None] * part_ids[None, :], part_count)
    freq_real = contract("kp,sepbc->sekbc", part_cos, real_part) + contract(
        "kp,sepbc->sekbc", part_sin, imag_part
    )
    freq_imag = contract("kp,sepbc->sekbc", part_cos, imag_part) - contract(
        "kp,sepbc->sekbc", part_sin, real_part
    )
    twist_cos, twist_sin = angles(part_ids[:, None] * row_ids[None, :], seq_length)
    twist_cos = twist_cos[None, None, :, :, None]
    twist_sin = twist_sin[None, None, :, :, None]
    turned_real = freq_real * twist_cos + freq_imag * twist_sin
    turned_imag = freq_imag * twist_cos - freq_real * twist_sin
    regrouped = lax.all_to_all(
        jnp.stack([turned_real, turned_imag]), "ctx", split_axis=3, concat_axis=4, tiled=True
    )[:, :, :, 0]
    all_rows = jnp.arange(row_count, dtype=jnp.int32)
    row_cos, row_sin = angles(all_rows[:, None] * all_rows[None, :], row_count)
    spec_real = contract("kr,serc->sekc", row_cos, regrouped[0]) + contract(
        "kr,serc->sekc", row_sin, regrouped[1]
    )
    spec_imag = contract("kr,serc->sekc", row_cos, regrouped[1]) - contract(
        "kr,serc->sekc", row_sin, regrouped[0]
    )
    spectra = jnp.stack([spec_real, spec_imag])
    ordered = lax.all_to_all(spectra[:, :, :, None], "ctx", split_axis=4, concat_axis=3, tiled=True)
    product = lax.all_to_all(products(ordered), "ctx", split_axis=3, concat_axis=4, tiled=True)[
        :, :, :, 0
    ]
    inv_real = contract("rk,sekc->serc", row_cos, product[0]) - contract(
        "rk,sekc->serc", row_sin, product[1]
    )
    inv_imag = contract("rk,sekc->serc", row_cos, product[1]) + contract(
        "rk,sekc->serc", row_sin, product[0]
    )
    back_cos, back_sin = angles(all_rows * position, seq_length)
    back_cos = back_cos[None, None, :, None]
    back_sin = back_sin[None, None, :, None]
    reverted_real = inv_real * back_cos - inv_imag * back_sin
    reverted_imag = inv_imag * back_cos + inv_real * back_sin
    returned = lax.all_to_all(
        jnp.stack([reverted_real, reverted_imag])[:, :, :, None],
        "ctx",
        split_axis=4,
        concat_axis=3,
        tiled=True,
    )
    out_real = contract("pk,sekbc->sepbc", part_cos, returned[0]) - contract(
        "pk,sekbc->sepbc", part_sin, returned[1]
    )
    out_imag = contract("pk,sekbc->sepbc", part_cos, returned[1]) + contract(
        "pk,sekbc->sepbc", part_sin, returned[0]
    )
    combined = (out_real[:, 0] + out_real[:, 1] * half_cos - out_imag[:, 1] * half_sin) / (
        2.0 * seq_length
    )
    collected = lax.all_to_all(combined, "ctx", split_axis=1, concat_axis=2, tiled=True)
    return collected[:, 0]


def shards(out_grad, gate_act, key_act, value_act, filter_taps, out_weight):
    row_count, chan_count = gate_act.shape
    part_count = lax.axis_size("ctx")
    position = lax.axis_index("ctx")
    seq_length = row_count * part_count
    grad_mix = lax.dot_general(
        lax.all_gather(out_grad, "tp", axis=1, tiled=True),
        out_weight,
        (((1,), (1,)), ((), ())),
        preferred_element_type=jnp.float32,
    ).astype(jnp.bfloat16)
    mixed_full = grad_mix.astype(jnp.float32)
    gate_full = gate_act.astype(jnp.float32)
    key_full = key_act.astype(jnp.float32)
    value_full = value_act.astype(jnp.float32)
    inner_prod = key_full * value_full
    tap_scale = 1.0 / math.sqrt(seq_length)
    grad_conv = mixed_full * gate_full
    signals = jnp.stack([inner_prod, filter_taps * tap_scale, grad_conv])
    result = token_path(signals, part_count, position, seq_length)
    grad_gate = (mixed_full * result[0]).astype(jnp.bfloat16)
    grad_key = (result[1] * value_full).astype(jnp.bfloat16)
    grad_value = (result[1] * key_full).astype(jnp.bfloat16)
    grad_taps = result[2] * tap_scale
    return (grad_gate, grad_key, grad_value, grad_taps)


def solution(mesh):
    in_specs = (
        P("ctx", "tp"),
        P("ctx", "tp"),
        P("ctx", "tp"),
        P("ctx", "tp"),
        P("ctx", "tp"),
        P("tp", None),
    )
    out_specs = (P("ctx", "tp"), P("ctx", "tp"), P("ctx", "tp"), P("ctx", "tp"))
    return jax.shard_map(shards, mesh=mesh, in_specs=in_specs, out_specs=out_specs, check_vma=False)
```

profile of v0, /device:TPU:32, one launch (start us, length us, event | category | flops | bytes accessed | tf_op | source)
XLA Modules:
  0.0 580.0 jit_solution(314780905951756966)
XLA Ops:
  7.2 0.0 all-gather.2.cloned.1.call-start
  7.2 0.7 all-gather.2.cloned.1.call-update
  7.9 1.4 fusion.41
  9.3 0.0 copy-start.2
  9.3 38.6 %all-gather.2.cloned.1.call-done = bf16[256,4096]{1,0:T(8,128)(2,1)} async-done(((bf16[256,512]{1,0:T(8,128)(2,1)}), bf16[256,4096]{1,0:T(8,128)(2,1)}) %all-gather.2.cloned.1.call-update) | async-done | bytes 2097168 | tf_op jit(solution)/shard_map/all_gather | solution.py:109
  47.9 4.1 fusion.37
  52.0 0.0 copy-done.2
  52.0 0.1 multiply_bitcast_fusion
  52.1 0.1 maximum_bitcast_fusion.4
  52.2 2.8 copy.126
  55.0 8.6 %all-to-all-start = ((f32[3,1,256,512]{3,1,0,2:T(1,128)}), f32[3,1,256,512]{3,1,0,2:T(1,128)S(1)}, u32[]{:S(2)}, u32[]{:S(2)}) async-start(f32[3,1,256,512]{3,1,0,2:T(1,128)} %copy.126), calls=%async_computation | async-start | bytes 3145728 | tf_op jit(solution)/shard_map/all_to_all | solution.py:35
  63.7 0.1 fusion.105
  63.8 21.4 %all-to-all-done = f32[3,1,256,512]{3,1,0,2:T(1,128)S(1)} async-done(((f32[3,1,256,512]{3,1,0,2:T(1,128)}), f32[3,1,256,512]{3,1,0,2:T(1,128)S(1)}, u32[]{:S(2)}, u32[]{:S(2)}) %all-to-all-start) | async-done | bytes 1572896 | tf_op jit(solution)/shard_map/all_to_all | solution.py:35
  85.2 0.1 copy.294
  85.3 3.2 fusion.35
  88.5 3.2 fusion.36
  91.7 1.0 fusion.185
  92.7 3.6 fusion.26
  96.3 4.7 fusion.5
  101.0 1.3 pad_maximum_fusion
  102.4 3.6 copy.131
  106.0 77.9 %all_to_all.27 = f32[2,3,2,32,8,512]{5,4,2,1,0,3:T(8,128)S(1)} all-to-all(f32[2,3,2,32,8,512]{5,4,2,1,0,3:T(8,128)S(1)} %copy.131), channel_id=1, replica_groups=mesh['ctx'=32,'tp'=8] {'ctx'}, dimensions={3} | all-to-all | bytes 12582912 | tf_op jit(solution)/shard_map/all_to_all | solution.py:56
  183.9 1.4 fusion.184
  185.3 6.3 %fusion.13 = f32[3,2,512,256]{3,2,1,0:T(8,128)S(1)} fusion(f32[1,3,2,32,8,512]{5,4,2,1,0,3:T(8,128)S(1)} %get-tuple-element.22), kind=kOutput, calls=%fused_computation.37 | convolution fusion | flops 2416836608 | bytes 6291456 | tf_op jit(solution)/shard_map/kr,serc->sekc/dot_general | solution.py:15
  191.6 6.5 %fusion.12 = f32[3,2,512,256]{3,2,1,0:T(8,128)S(1)} fusion(f32[1,3,2,32,8,512]{5,4,2,1,0,3:T(8,128)S(1)} %get-tuple-element.22), kind=kOutput, calls=%fused_computation.36 | convolution fusion | flops 2416836608 | bytes 6291456 | tf_op jit(solution)/shard_map/kr,serc->sekc/dot_general | solution.py:15
  198.1 6.3 %add_bitcast_fusion.2 = f32[1,3,2,256,512]{3,4,2,1,0:T(8,128)S(1)} fusion(f32[3,2,512,256]{3,2,1,0:T(8,128)S(1)} %fusion.13, f32[1,3,2,32,8,512]{5,4,2,1,0,3:T(8,128)S(1)} %get-tuple-element.21), kind=kOutput, calls=%fused_computation.35 | convolution fusion | flops 2417623040 | bytes 9437184 | tf_op jit(solution)/shard_map/kr,serc->sekc/dot_general | solution.py:15
  204.3 6.5 %subtract_bitcast_fusion.2 = f32[1,3,2,256,512]{3,4,2,1,0:T(8,128)S(1)} fusion(f32[3,2,512,256]{3,2,1,0:T(8,128)S(1)} %fusion.12, f32[1,3,2,32,8,512]{5,4,2,1,0,3:T(8,128)S(1)} %get-tuple-element.21), kind=kOutput, calls=%fused_computation.34 | convolution fusion | flops 2417623040 | bytes 9437184 | tf_op jit(solution)/shard_map/kr,serc->sekc/dot_general | solution.py:15
  210.9 3.5 maximum_bitcast_fusion
  214.3 10.4 %copy.138 = f32[2,3,2,1,256,512]{5,2,1,0,3,4:T(2,128)} copy(f32[2,3,2,1,256,512]{4,5,2,1,0,3:T(8,128)} %maximum_bitcast_fusion) | data formatting | bytes 12582912 | tf_op jit(solution)/shard_map/broadcast_in_dim | solution.py:68
  224.7 76.5 %all_to_all.28 = f32[2,3,2,1,256,512]{5,2,1,0,3,4:T(2,128)S(1)} all-to-all(f32[2,3,2,1,256,512]{5,2,1,0,3,4:T(2,128)} %copy.138), channel_id=1, replica_groups=mesh['ctx'=32,'tp'=8] {'ctx'}, dimensions={4} | all-to-all | bytes 12582912 | tf_op jit(solution)/shard_map/all_to_all | solution.py:68
  301.2 1.1 slice.120
  302.3 0.6 copy.293
  302.9 2.1 fusion.183
  305.0 1.2 multiply_subtract_fusion.2
  306.2 0.6 maximum_bitcast_fusion.2
  306.8 0.6 maximum_bitcast_fusion.3
  307.4 0.7 pad_maximum_fusion.1
  308.1 3.3 copy.145
  311.4 7.0 %all-to-all-start.3 = ((f32[2,3,2,32,8,512]{5,4,2,1,0,3:T(8,128)}), f32[2,3,2,32,8,512]{5,4,2,1,0,3:T(8,128)}, u32[]{:S(2)}, u32[]{:S(2)}) async-start(f32[2,3,2,32,8,512]{5,4,2,1,0,3:T(8,128)} %copy.145), calls=%async_computation.3 | async-start | bytes 12582912 | tf_op jit(solution)/shard_map/all_to_all | solution.py:69
  318.4 0.1 fusion.111
  318.4 76.5 %all-to-all-done.3 = f32[2,3,2,32,8,512]{5,4,2,1,0,3:T(8,128)} async-done(((f32[2,3,2,32,8,512]{5,4,2,1,0,3:T(8,128)}), f32[2,3,2,32,8,512]{5,4,2,1,0,3:T(8,128)}, u32[]{:S(2)}, u32[]{:S(2)}) %all-to-all-start.3) | async-done | bytes 6291488 | tf_op jit(solution)/shard_map/all_to_all | solution.py:69
  394.9 3.6 fusion.182
  398.5 6.3 %fusion.17 = f32[3,2,512,256]{3,2,1,0:T(8,128)S(1)} fusion(f32[1,3,2,32,8,512]{5,4,2,1,0,3:T(8,128)S(1)} %get-tuple-element.11), kind=kOutput, calls=%fused_computation.41 | convolution fusion | flops 2416836608 | bytes 6291456 | tf_op jit(solution)/shard_map/rk,sekc->serc/dot_general | solution.py:15
  404.8 6.5 %fusion.16 = f32[3,2,512,256]{3,2,1,0:T(8,128)S(1)} fusion(f32[1,3,2,32,8,512]{5,4,2,1,0,3:T(8,128)S(1)} %get-tuple-element.11), kind=kOutput, calls=%fused_computation.40 | convolution fusion | flops 2416836608 | bytes 6291456 | tf_op jit(solution)/shard_map/rk,sekc->serc/dot_general | solution.py:15
  411.3 6.3 %fusion.28 = f32[3,2,512,256]{3,2,1,0:T(8,128)S(1)} fusion(f32[3,2,512,256]{3,2,1,0:T(8,128)S(1)} %fusion.17, f32[1,3,2,32,8,512]{5,4,2,1,0,3:T(8,128)S(1)} %get-tuple-element.10), kind=kOutput, calls=%fused_computation.48 | convolution fusion | flops 2417623040 | bytes 9437184 | tf_op jit(solution)/shard_map/rk,sekc->serc/dot_general | solution.py:15
  417.6 7.3 %subtract_bitcast_fusion.1 = (f32[1,3,2,256,512]{3,4,2,1,0:T(8,128)S(1)}, f32[1,3,2,256,512]{3,4,2,1,0:T(8,128)S(1)}) fusion(f32[3,2,512,256]{3,2,1,0:T(8,128)S(1)} %fusion.28, f32[256]{0:T(256)S(1)} %get-tuple-element.38, f32[256]{0:T(256)S(1)} %get-tuple-element.39, f32[3,2,512,256]{3,2,1,0:T(8,128)S(1)} %fusion.16, ...), kind=kOutput, calls=%fused_computation.33 | convolution fusion | flops 2422341632 | bytes 15730688 | tf_op jit(solution)/shard_map/rk,sekc->serc/dot_general | solution.py:15
  424.9 3.5 maximum_bitcast_fusion.1
  428.4 10.4 %copy.152 = f32[2,3,2,1,256,512]{5,2,1,0,3,4:T(2,128)} copy(f32[2,3,2,1,256,512]{4,5,2,1,0,3:T(8,128)} %maximum_bitcast_fusion.1) | data formatting | bytes 12582912 | tf_op jit(solution)/shard_map/broadcast_in_dim | solution.py:84
  438.8 80.0 %all_to_all.29 = f32[2,3,2,1,256,512]{5,2,1,0,3,4:T(2,128)S(1)} all-to-all(f32[2,3,2,1,256,512]{5,2,1,0,3,4:T(2,128)} %copy.152), channel_id=1, replica_groups=mesh['ctx'=32,'tp'=8] {'ctx'}, dimensions={4} | all-to-all | bytes 12582912 | tf_op jit(solution)/shard_map/all_to_all | solution.py:83
  518.7 2.2 fusion.181
  520.9 0.6 copy.291
  521.5 5.2 fusion.8
  526.7 0.6 copy.292
  527.3 5.4 fusion
  532.7 5.5 subtract_bitcast_fusion
  538.3 5.5 add_bitcast_fusion
  543.8 0.4 fusion.32
  544.2 0.0 copy-start
  544.2 0.0 copy-start.1
  544.3 0.9 copy.162
  545.2 25.9 %all_to_all.60 = f32[3,32,8,512]{3,2,0,1:T(8,128)S(1)} all-to-all(f32[3,32,8,512]{3,2,0,1:T(8,128)S(1)} %copy.162), channel_id=1, replica_groups=mesh['ctx'=32,'tp'=8] {'ctx'}, dimensions={1} | all-to-all | bytes 3145728 | tf_op jit(solution)/shard_map/all_to_all | solution.py:99
  571.1 0.0 copy-done
  571.1 1.1 fusion.40
  572.1 0.8 fusion.44
  (3 shorter events, 0.0 us)
Async XLA Ops:
  7.2 40.8 %all-gather.2.cloned.1.call-start = ((), (), s32[]{:S(2)}) async-start(), calls=%async_computation.6 | async-start | bytes 2359296 | tf_op jit(solution)/shard_map/all_gather | solution.py:109
  9.3 42.8 %copy-start.2 = (bf16[256,512]{1,0:T(8,128)(2,1)S(1)}, bf16[256,512]{1,0:T(8,128)(2,1)}, u32[]{:S(2)}) copy-start(bf16[256,512]{1,0:T(8,128)(2,1)} %param.7) | copy-start | bytes 786436
  55.0 30.2 %all-to-all-start = ((f32[3,1,256,512]{3,1,0,2:T(1,128)}), f32[3,1,256,512]{3,1,0,2:T(1,128)S(1)}, u32[]{:S(2)}, u32[]{:S(2)}) async-start(f32[3,1,256,512]{3,1,0,2:T(1,128)} %copy.126), calls=%async_computation | async-start | bytes 3145728 | tf_op jit(solution)/shard_map/all_to_all | solution.py:35
  311.4 83.5 %all-to-all-start.3 = ((f32[2,3,2,32,8,512]{5,4,2,1,0,3:T(8,128)}), f32[2,3,2,32,8,512]{5,4,2,1,0,3:T(8,128)}, u32[]{:S(2)}, u32[]{:S(2)}) async-start(f32[2,3,2,32,8,512]{5,4,2,1,0,3:T(8,128)} %copy.145), calls=%async_computation.3 | async-start | bytes 12582912 | tf_op jit(solution)/shard_map/all_to_all | solution.py:69
  544.2 26.9 %copy-start = (bf16[256,512]{1,0:T(8,128)(2,1)S(1)}, bf16[256,512]{1,0:T(8,128)(2,1)}, u32[]{:S(2)}) copy-start(bf16[256,512]{1,0:T(8,128)(2,1)} %param.8) | copy-start | bytes 786436
  544.2 26.8 %copy-start.1 = (bf16[256,512]{1,0:T(8,128)(2,1)S(1)}, bf16[256,512]{1,0:T(8,128)(2,1)}, u32[]{:S(2)}) copy-start(bf16[256,512]{1,0:T(8,128)(2,1)} %param.9) | copy-start | bytes 786436
Sparse Core Ops, SparseCore 0:
  9.8 38.0 all-gather.1
where the time goes:
time: 587 us; the launch traced here: 580 us
  blocking collectives  260 us (44%)
  waiting for transfers between devices  137 us (23%)
  matrix products  92.4 us (16%)
  local copies, waits for them, and re-layouts  43.6 us (7%)
  other arithmetic  16.3 us (3%)
  starting transfers between devices  15.6 us (3%)
  between operations  14.6 us (2%)
    dot_general x16, matrix products, contract(): return jnp.einsum(form, table, data, precision=lax.Precision.HIGHEST)  88.3 us
    all_to_all x1, blocking collectives, token_path(): lax.all_to_all(jnp.stack([reverted_real, reverted_imag])[:, :, :, None],...  80 us
    all_to_all x1, blocking collectives, token_path(): lax.all_to_all(jnp.stack([turned_real, turned_imag]), 'ctx', split_axis=3...  77.9 us
    all_to_all x1, waiting for transfers between devices, token_path(): lax.all_to_all(products(ordered), 'ctx', split_axis=3, concat_axis=4, til...  76.5 us
    all_to_all x1, blocking collectives, token_path(): lax.all_to_all(spectra[:, :, :, None], 'ctx', split_axis=4, concat_axis=3...  76.5 us
    all_gather x1, waiting for transfers between devices, shards(): lax.all_gather(out_grad, 'tp', axis=1, tiled=True)  38.6 us
    all_to_all x1, blocking collectives, token_path(): lax.all_to_all(combined, 'ctx', split_axis=1, concat_axis=2, tiled=True)  25.9 us
    all_to_all x1, waiting for transfers between devices, token_path(): lax.all_to_all(signals[:, None], 'ctx', split_axis=2, concat_axis=1, tile...  21.4 us
  transfers between devices with their start and end apart: 3, of which 3 were waited for; matrix products, arithmetic and copies ran while one was open for 0% of the time, Pallas kernels for 0%

commit v1 on v0

v1 whole, which is shorter than its diff:
```python
import math

import jax
import jax.numpy as jnp
import ml_dtypes
import numpy as np
from jax import lax
from jax.experimental import pallas as pl
from jax.experimental.pallas import tpu as pltpu
from jax.sharding import PartitionSpec as P

BF = jnp.bfloat16
F32 = jnp.float32
PARTS = 32
ROWS = 256
CHANS = 16
TOKENS = PARTS * ROWS
CHUNKS = 4
STEP = PARTS // CHUNKS
HALF = STEP * CHANS


def tables():
    k1 = np.arange(PARTS)
    r = np.arange(ROWS)
    first = 2.0 * np.pi * (((4 * k1[:, None] + 1) * k1[None, :]) % (4 * PARTS)) / (4 * PARTS)
    twist = 2.0 * np.pi * (((4 * k1[:, None] + 1) * r[None, :]) % (4 * TOKENS)) / (4 * TOKENS)
    second = 2.0 * np.pi * ((r[:, None] * r[None, :]) % ROWS) / ROWS
    eye = np.eye(CHANS)
    rows = []
    for i in range(CHUNKS):
        part = first[i * STEP : (i + 1) * STEP]
        rows += [np.kron(np.cos(part), eye), np.kron(-np.sin(part), eye)]
    spread = np.concatenate(rows, 0)
    cos, sin = np.cos(second), np.sin(second)
    ahead = np.block([[cos, -sin], [sin, cos]])
    back = np.block([[cos, sin], [-sin, cos]])
    wide = lambda a: np.ascontiguousarray(
        np.broadcast_to(a[:, None, :], (PARTS, 8, ROWS))
    ).astype(np.float32)
    half = lambda a: np.ascontiguousarray(a).astype(ml_dtypes.bfloat16)
    return (
        half(spread),
        half(spread.T),
        half(ahead),
        half(back),
        wide(np.cos(twist)),
        wide(np.sin(twist)),
    )


def dot(a, b):
    return lax.dot_general(a, b, (((1,), (0,)), ((), ())), preferred_element_type=F32)


def dot_t(a, b):
    return lax.dot_general(a, b, (((1,), (1,)), ((), ())), preferred_element_type=F32)


def turn(re, im, cos, sin):
    re = re.reshape(STEP, 2, 8, ROWS)
    im = im.reshape(STEP, 2, 8, ROWS)
    cos, sin = cos[:, None], sin[:, None]
    out_re = (re * cos - im * sin).astype(BF).reshape(HALF, ROWS)
    out_im = (im * cos + re * sin).astype(BF).reshape(HALF, ROWS)
    return out_re, out_im


def forward(signal, i, spread, ahead, cos, sin):
    a = dot(spread[2 * HALF * i : 2 * HALF * (i + 1), :], signal)
    part = slice(i * STEP, (i + 1) * STEP)
    re, im = turn(a[:HALF], a[HALF:], cos[part], -sin[part])
    return dot(jnp.concatenate([re, im], 1), ahead[...])


def inverse(re, im, i, back, cos, sin, held, slot):
    z = dot(jnp.concatenate([re.astype(BF), im.astype(BF)], 1), back[...])
    part = slice(i * STEP, (i + 1) * STEP)
    re, im = turn(z[:, :ROWS], z[:, ROWS:], cos[part], sin[part])
    held[slot, 2 * HALF * i : 2 * HALF * i + HALF, :] = re
    held[slot, 2 * HALF * i + HALF : 2 * HALF * (i + 1), :] = im


SCALE = 1.0 / (math.sqrt(TOKENS) * TOKENS)


def collect(gather, held, slot):
    return (dot(gather[...], held[slot]) * SCALE).astype(BF).reshape(PARTS, CHANS, ROWS)


def prepare_kernel(key, value, taps, out):
    inner = key[...].astype(F32) * value[...].astype(F32)
    out[:, 0] = inner.T.astype(BF).reshape(PARTS, CHANS, ROWS)
    out[:, 1] = taps[...].T.astype(BF).reshape(PARTS, CHANS, ROWS)


def early_kernel(got, spread, gather, ahead, back, cos, sin, spec, conv, held):
    inner = got[:, 0].reshape(PARTS * CHANS, ROWS)
    taps = got[:, 1].reshape(PARTS * CHANS, ROWS)
    for i in range(CHUNKS):
        x = forward(inner, i, spread, ahead, cos, sin)
        h = forward(taps, i, spread, ahead, cos, sin)
        spec[0, HALF * i : HALF * (i + 1), :] = x
        spec[1, HALF * i : HALF * (i + 1), :] = h
        xr, xi, hr, hi = x[:, :ROWS], x[:, ROWS:], h[:, :ROWS], h[:, ROWS:]
        inverse(hr * xr - hi * xi, hr * xi + hi * xr, i, back, cos, sin, held, 0)
    conv[...] = collect(gather, held, 0)


def late_kernel(got, spec, conv, spread, gather, ahead, back, cos, sin, out, held):
    out[:, 0] = conv[...]
    grad = got[...].reshape(PARTS * CHANS, ROWS)
    for i in range(CHUNKS):
        g = forward(grad, i, spread, ahead, cos, sin)
        rows = slice(HALF * i, HALF * (i + 1))
        gr, gi = g[:, :ROWS], g[:, ROWS:]
        xr, xi = spec[0, rows, :ROWS], spec[0, rows, ROWS:]
        hr, hi = spec[1, rows, :ROWS], spec[1, rows, ROWS:]
        inverse(hr * gr + hi * gi, hr * gi - hi * gr, i, back, cos, sin, held, 0)
        inverse(xr * gr + xi * gi, xr * gi - xi * gr, i, back, cos, sin, held, 1)
    out[:, 1] = collect(gather, held, 0)
    out[:, 2] = collect(gather, held, 1)


def first_mix_kernel(ids, weight, *refs):
    blocks, out = refs[:-1], refs[-1]
    total = None
    for n, block in enumerate(blocks):
        width = block.shape[1]
        columns = pl.ds(pl.multiple_of(ids[n] * width, width), width)
        term = dot_t(block[...], weight[:, columns])
        total = term if total is None else total + term
    out[...] = total


def last_mix_kernel(ids, total, far, far_pair, weight, weight_pair, gate, mix, out):
    del ids
    sums = total[...] + dot_t(far[...], weight[...]) + dot_t(far_pair[...], weight_pair[...])
    mixed = sums.astype(BF)
    mix[...] = mixed
    grad = mixed.astype(F32) * gate[...].astype(F32)
    out[...] = grad.T.astype(BF).reshape(PARTS, CHANS, ROWS)


def finish_kernel(got, mix, key, value, grad_gate, grad_key, grad_value, grad_taps):
    def result(slot):
        return got[:, slot].reshape(PARTS * CHANS, ROWS).astype(F32).T

    grad_gate[...] = (mix[...].astype(F32) * result(0)).astype(BF)
    inner = result(1)
    grad_key[...] = (inner * value[...].astype(F32)).astype(BF)
    grad_value[...] = (inner * key[...].astype(F32)).astype(BF)
    grad_taps[...] = result(2)


PARAMS = pltpu.CompilerParams(vmem_limit_bytes=48 * 1024 * 1024)


def call(kernel, outs, *args, scratch=(), flops=0):
    nbytes = sum(a.size * a.dtype.itemsize for a in (*args, *jax.tree.leaves(outs)))
    return pl.pallas_call(
        kernel,
        out_shape=outs,
        scratch_shapes=scratch,
        compiler_params=PARAMS,
        cost_estimate=pl.CostEstimate(flops=flops, bytes_accessed=nbytes, transcendentals=0),
    )(*args)


def shape(dims, dtype=BF):
    return jax.ShapeDtypeStruct(dims, dtype)


def shards(out_grad, gate_act, key_act, value_act, filter_taps, out_weight):
    count = lax.axis_size("tp")
    me = lax.axis_index("tp")

    def ring(block, steps):
        return lax.ppermute(block, "tp", [(i, (i + steps) % count) for i in range(count)])

    def swap(block):
        return lax.ppermute(block, "tp", [(i, i ^ 1) for i in range(count)])

    def exchange(block):
        return lax.all_to_all(block, "ctx", split_axis=0, concat_axis=0, tiled=True)

    spread, gather, ahead, back, cos, sin = (jnp.asarray(t) for t in tables())
    block = (PARTS, CHANS, ROWS)
    rows, chans = gate_act.shape

    right = ring(out_grad, 2)
    left = ring(out_grad, -2)
    far = ring(out_grad, 4)
    pair = swap(out_grad)

    sent = call(prepare_kernel, shape((PARTS, 2, CHANS, ROWS)), key_act, value_act, filter_taps)
    got = exchange(sent)
    held = lambda n: [pltpu.VMEM((n, 2 * PARTS * CHANS, ROWS), BF)]
    spec, conv = call(
        early_kernel,
        (shape((2, PARTS * CHANS, 2 * ROWS), F32), shape(block)),
        got, spread, gather, ahead, back, cos, sin,
        scratch=held(1), flops=1_600_000_000,
    )

    offsets = jnp.array([0, 0, -2, -2, 2, 2, 4, 4], jnp.int32)
    flips = jnp.array([0, 1, 0, 1, 0, 1, 0, 1], jnp.int32)
    ids = ((me ^ flips) + offsets) % count
    smem = pl.BlockSpec(memory_space=pltpu.SMEM)
    blocks = (out_grad, pair, right, swap(right), left, swap(left))
    total = pl.pallas_call(
        first_mix_kernel,
        out_shape=shape((rows, chans), F32),
        in_specs=[smem] + [pl.BlockSpec(memory_space=pltpu.VMEM)] * (1 + len(blocks)),
        compiler_params=PARAMS,
        cost_estimate=pl.CostEstimate(flops=800_000_000, bytes_accessed=6_000_000, transcendentals=0),
    )(ids, out_weight, *blocks)

    whole = lambda dims: pl.BlockSpec(dims, lambda i, ids: (0,) * len(dims))
    mix, sent = pl.pallas_call(
        last_mix_kernel,
        out_shape=(shape((rows, chans)), shape(block)),
        grid_spec=pltpu.PrefetchScalarGridSpec(
            num_scalar_prefetch=1,
            grid=(1,),
            in_specs=[
                whole((rows, chans)),
                whole((rows, chans)),
                whole((rows, chans)),
                pl.BlockSpec((chans, chans), lambda i, ids: (0, ids[6])),
                pl.BlockSpec((chans, chans), lambda i, ids: (0, ids[7])),
                whole((rows, chans)),
            ],
            out_specs=[whole((rows, chans)), whole(block)],
        ),
        compiler_params=PARAMS,
        cost_estimate=pl.CostEstimate(flops=270_000_000, bytes_accessed=3_000_000, transcendentals=0),
    )(ids, total, far, swap(far), out_weight, out_weight, gate_act)

    got = exchange(sent)
    sent = call(
        late_kernel,
        shape((PARTS, 3, CHANS, ROWS)),
        got, spec, conv, spread, gather, ahead, back, cos, sin,
        scratch=held(2), flops=1_600_000_000,
    )
    got = exchange(sent)
    return call(
        finish_kernel,
        (shape((rows, chans)), shape((rows, chans)), shape((rows, chans)), shape((rows, chans), F32)),
        got, mix, key_act, value_act,
    )


def solution(mesh):
    in_specs = (
        P("ctx", "tp"),
        P("ctx", "tp"),
        P("ctx", "tp"),
        P("ctx", "tp"),
        P("ctx", "tp"),
        P("tp", None),
    )
    out_specs = (P("ctx", "tp"), P("ctx", "tp"), P("ctx", "tp"), P("ctx", "tp"))
    return jax.shard_map(shards, mesh=mesh, in_specs=in_specs, out_specs=out_specs, check_vma=False)
```

time: 587 us -> 103 us (0.18)
  the two profiles are of different devices: /device:TPU:32 before, /device:TPU:64 now
where the time goes in v1:
time: 103 us; the launch traced here: 102 us
  waiting for transfers between devices  26.3 us (26%)
  starting transfers between devices  25.7 us (25%)
  blocking collectives  20.1 us (20%)
  Pallas kernels  17.7 us (17%)
  local copies, waits for them, and re-layouts  10.8 us (10%)
    ppermute x3, waiting for transfers between devices, ring(): lax.ppermute(block, 'tp', [(i, (i + steps) % count) for i in range(count)])  24.2 us
    all_to_all x1, blocking collectives, exchange(): return lax.all_to_all(block, 'ctx', split_axis=0, concat_axis=0, tiled=True)  20.1 us
    all_to_all x2, starting transfers between devices, exchange(): return lax.all_to_all(block, 'ctx', split_axis=0, concat_axis=0, tiled=True)  17 us
    pallas_call x4, Pallas kernels, call(): pl.pallas_call(kernel, out_shape=outs, scratch_shapes=scratch, compiler_p...  12.2 us
    unnamed x42, local copies, waits for them, and re-layouts  10.8 us
    ppermute x3, starting transfers between devices, ring(): lax.ppermute(block, 'tp', [(i, (i + steps) % count) for i in range(count)])  8.7 us
    pallas_call x1, Pallas kernels, shards(): pl.pallas_call(first_mix_kernel, out_shape=shape((rows, chans), F32), in_...  3.2 us
    pallas_call x1, Pallas kernels, shards(): pl.pallas_call(last_mix_kernel, out_shape=(shape((rows, chans)), shape(bl...  2.36 us
  transfers between devices with their start and end apart: 9, of which 4 were waited for; matrix products, arithmetic and copies ran while one was open for 1% of the time, Pallas kernels for 10%

profile of v1, /device:TPU:64, one launch (start us, length us, event | category | flops | bytes accessed | tf_op | source)
XLA Modules:
  0.0 102.1 jit_solution(11809041096192619475)
XLA Ops:
  0.6 0.0 copy-start.3
  0.6 0.9 copy-done.3
  1.6 0.0 copy-start.5
  1.6 0.9 copy-done.5
  2.5 0.0 copy-start.7
  2.5 1.0 %copy-done.7 = f32[256,512]{1,0:T(8,128)S(1)} copy-done((f32[256,512]{1,0:T(8,128)S(1)}, f32[256,512]{1,0:T(8,128)}, u32[]{:S(2)}) %copy-start.7) | copy-done | bytes 524312
  3.6 0.0 copy-start.17
  3.6 1.0 shard_map.167
  4.6 8.8 %all-to-all-start.1 = ((bf16[32,2,16,256]{3,2,1,0:T(8,128)(2,1)}), bf16[32,2,16,256]{3,2,1,0:T(8,128)(2,1)}, u32[]{:S(2)}, u32[]{:S(2)}) async-start(bf16[32,2,16,256]{3,2,1,0:T(8,128)(2,1)} %shard_map.167), calls=%async_computation.1 | async-start | bytes 1048576 | tf_op jit(solution)/shard_map/all_to_all | solution.py:185
  13.4 0.1 collective-permute-start.3
  13.5 4.1 %collective-permute-start.1 = (bf16[256,512]{1,0:T(8,128)(2,1)}, bf16[256,512]{1,0:T(8,128)(2,1)S(1)}, u32[]{:S(2)}, u32[]{:S(2)}) collective-permute-start(bf16[256,512]{1,0:T(8,128)(2,1)} %refs_0_.1), channel_id=1, source_target_pairs={{0,2},{1,3},{2,4},{3,5},{4,6},{5,7},{6,0},{7,1},{8,10},{9,11},{10,... | collective-permute-start | bytes 786440 | tf_op jit(solution)/shard_map/ppermute | solution.py:179
  17.6 4.5 %collective-permute-start.5 = (bf16[256,512]{1,0:T(8,128)(2,1)}, bf16[256,512]{1,0:T(8,128)(2,1)}, u32[]{:S(2)}, u32[]{:S(2)}) collective-permute-start(bf16[256,512]{1,0:T(8,128)(2,1)} %refs_0_.1), channel_id=1, source_target_pairs={{0,4},{1,5},{2,6},{3,7},{4,0},{5,1},{6,2},{7,3},{8,12},{9,13},{10,... | collective-permute-start | bytes 786440 | tf_op jit(solution)/shard_map/ppermute | solution.py:179
  22.1 0.0 collective-permute-start
  22.1 1.6 %collective-permute-done.3.refs_4_ = bf16[256,512]{1,0:T(8,128)(2,1)S(1)} collective-permute-done((bf16[256,512]{1,0:T(8,128)(2,1)}, bf16[256,512]{1,0:T(8,128)(2,1)S(1)}, u32[]{:S(2)}, u32[]{:S(2)}) %collective-permute-start.3) | collective-permute-done | bytes 262176 | tf_op jit(solution)/shard_map/ppermute | solution.py:179
  23.7 0.0 collective-permute-start.4
  23.7 13.3 %collective-permute-done.1.refs_2_ = bf16[256,512]{1,0:T(8,128)(2,1)S(1)} collective-permute-done((bf16[256,512]{1,0:T(8,128)(2,1)}, bf16[256,512]{1,0:T(8,128)(2,1)S(1)}, u32[]{:S(2)}, u32[]{:S(2)}) %collective-permute-start.1) | collective-permute-done | bytes 262176 | tf_op jit(solution)/shard_map/ppermute | solution.py:179
  36.9 0.0 collective-permute-start.2
  36.9 0.0 copy-start
  37.0 9.4 %collective-permute-done.5.far = bf16[256,512]{1,0:T(8,128)(2,1)} collective-permute-done((bf16[256,512]{1,0:T(8,128)(2,1)}, bf16[256,512]{1,0:T(8,128)(2,1)}, u32[]{:S(2)}, u32[]{:S(2)}) %collective-permute-start.5) | collective-permute-done | bytes 262176 | tf_op jit(solution)/shard_map/ppermute | solution.py:179
  46.3 0.0 collective-permute-start.6
  46.3 0.7 and_select_fusion.ids
  47.0 0.0 collective-permute-done.refs_1_
  47.0 0.0 collective-permute-done.4.refs_5_
  47.0 0.0 collective-permute-done.2.refs_3_
  47.0 0.0 copy-start.16
  47.0 0.9 copy-done.16
  48.0 3.2 %shard_map.165.total = f32[256,512]{1,0:T(8,128)S(1)} custom-call(s32[8]{0:T(128)S(1)} %and_select_fusion.ids, bf16[512,4096]{1,0:T(8,128)(2,1)} %weight_pair.1, bf16[256,512]{1,0:T(8,128)(2,1)S(1)} %copy-done.16, bf16[256,512]{1,0:T(8,128)(2,1)S(1)} %collective-permute-done.refs_1_, bf16[256,512]{1,0:T(8,128)(2,1)S(1)} %collective-permute-done.1.refs_2_, ...), custom_call_target="tpu_custom_call" | custom-call | flops 800000000 | bytes 6000000 | tf_op jit(solution)/shard_map/pallas_call | solution.py:211
  51.2 0.0 copy-start.1
  51.2 0.0 copy-start.2
  51.2 0.0 copy-start.8
  51.2 0.0 copy-start.9
  51.2 0.0 collective-permute-done.6.far_pair
  51.3 0.0 copy-done.17
  51.3 0.0 copy-done
  51.3 2.4 %shard_map.166 = (bf16[256,512]{1,0:T(8,128)(2,1)S(1)}, bf16[32,16,256]{2,1,0:T(8,128)(2,1)S(1)}) custom-call(s32[8]{0:T(128)S(1)} %and_select_fusion.ids, f32[256,512]{1,0:T(8,128)S(1)} %shard_map.165.total, bf16[256,512]{1,0:T(8,128)(2,1)} %collective-permute-done.5.far, bf16[256,512]{1,0:T(8,128)(2,1)S(1)} %collective-permute-done.6.far_pair, ...), custom_call_target="tpu_custom_call" | custom-call | flops 270000000 | bytes 3000000 | tf_op jit(solution)/shard_map/pallas_call | solution.py:220
  53.6 0.0 copy-start.18
  53.7 0.7 copy-done.18
  54.3 0.0 copy-start.19
  54.4 0.7 copy-done.19
  55.1 0.0 all-to-all-done.1.got
  55.1 8.2 %all-to-all-start = ((bf16[32,16,256]{2,1,0:T(8,128)(2,1)}), bf16[32,16,256]{2,1,0:T(8,128)(2,1)S(1)}, u32[]{:S(2)}, u32[]{:S(2)}) async-start(bf16[32,16,256]{2,1,0:T(8,128)(2,1)} %copy-done.18), calls=%async_computation | async-start | bytes 524288 | tf_op jit(solution)/shard_map/all_to_all | solution.py:185
  63.2 0.0 copy-done.1
  63.2 0.0 copy-done.2
  63.3 0.0 copy-done.8
  63.3 0.0 copy-done.9
  63.3 0.0 copy-start.10
  63.3 0.9 copy-done.10
  64.2 0.0 copy-start.12
  64.2 0.9 copy-done.12
  65.2 5.1 %shard_map.168 = (f32[2,512,512]{2,1,0:T(8,128)}, bf16[32,16,256]{2,1,0:T(8,128)(2,1)S(1)}) custom-call(bf16[32,2,16,256]{3,2,1,0:T(8,128)(2,1)} %all-to-all-done.1.got, bf16[1024,512]{1,0:T(8,128)(2,1)S(1)} %copy-done.2, bf16[512,1024]{1,0:T(8,128)(2,1)S(1)} %copy-done.1, bf16[512,512]{1,0:T(8,128)(2,1)S(1)} %copy-done.9, bf16[512,512]{1,0:T(8,128)(2,1)S(1)} %copy-done.8, ...), custom_call_target="tpu_custom_call" | custom-call | flops 1600000000 | bytes 6553600 | tf_op jit(solution)/shard_map/pallas_call | solution.py:161
  70.3 0.0 copy-start.14
  70.3 0.7 copy-done.14
  71.0 2.1 %all-to-all-done.got = bf16[32,16,256]{2,1,0:T(8,128)(2,1)S(1)} async-done(((bf16[32,16,256]{2,1,0:T(8,128)(2,1)}), bf16[32,16,256]{2,1,0:T(8,128)(2,1)S(1)}, u32[]{:S(2)}, u32[]{:S(2)}) %all-to-all-start) | async-done | bytes 262176 | tf_op jit(solution)/shard_map/all_to_all | solution.py:185
  73.0 0.0 copy-start.11
  73.0 0.9 copy-done.11
  74.0 0.9 copy-done.13
  74.9 0.0 copy-start.15
  74.9 0.9 copy-done.15
  75.9 4.8 %shard_map.169 = bf16[32,3,16,256]{3,2,1,0:T(8,128)(2,1)S(1)} custom-call(bf16[32,16,256]{2,1,0:T(8,128)(2,1)S(1)} %all-to-all-done.got, f32[2,512,512]{2,1,0:T(8,128)} %get-tuple-element.9.spec, bf16[32,16,256]{2,1,0:T(8,128)(2,1)S(1)} %copy-done.15, bf16[1024,512]{1,0:T(8,128)(2,1)S(1)} %copy-done.2, bf16[512,1024]{1,0:T(8,128)(2,1)S(1)} %copy-done.1, ...), custom_call_target="tpu_custom_call" | custom-call | flops 1600000000 | bytes 7077888 | tf_op jit(solution)/shard_map/pallas_call | solution.py:161
  80.7 20.1 %all_to_all.15.got = bf16[32,3,16,256]{3,2,1,0:T(8,128)(2,1)S(1)} all-to-all(bf16[32,3,16,256]{3,2,1,0:T(8,128)(2,1)S(1)} %shard_map.169), channel_id=1, replica_groups=mesh['ctx'=32,'tp'=8] {'ctx'}, dimensions={0} | all-to-all | bytes 1572864 | tf_op jit(solution)/shard_map/all_to_all | solution.py:185
  100.9 0.0 copy-done.4
  100.9 0.0 copy-done.6
  100.9 0.0 copy-done.20
  100.9 1.2 %shard_map.170 = (bf16[256,512]{1,0:T(8,128)(2,1)}, bf16[256,512]{1,0:T(8,128)(2,1)}, bf16[256,512]{1,0:T(8,128)(2,1)}, f32[256,512]{1,0:T(8,128)}) custom-call(bf16[32,3,16,256]{3,2,1,0:T(8,128)(2,1)S(1)} %all_to_all.15.got, bf16[256,512]{1,0:T(8,128)(2,1)S(1)} %copy-done.20, bf16[256,512]{1,0:T(8,128)(2,1)S(1)} %copy-done.4, bf16[256,512]{1,0:T(8,128)(2,1)S(1)} %copy-done.6), custom_call_target="tpu_custom_call" | custom-call | bytes 2883584 | tf_op jit(solution)/shard_map/pallas_call | solution.py:161
  (4 shorter events, 0.0 us)
Async XLA Ops:
  0.6 1.0 copy-start.3
  1.6 0.9 copy-start.5
  2.5 1.0 %copy-start.7 = (f32[256,512]{1,0:T(8,128)S(1)}, f32[256,512]{1,0:T(8,128)}, u32[]{:S(2)}) copy-start(f32[256,512]{1,0:T(8,128)} %taps.1) | copy-start | bytes 1572868
  3.6 47.7 %copy-start.17 = (bf16[256,512]{1,0:T(8,128)(2,1)S(1)}, bf16[256,512]{1,0:T(8,128)(2,1)}, u32[]{:S(2)}) copy-start(bf16[256,512]{1,0:T(8,128)(2,1)} %gate.1) | copy-start | bytes 786436
  4.6 50.5 %all-to-all-start.1 = ((bf16[32,2,16,256]{3,2,1,0:T(8,128)(2,1)}), bf16[32,2,16,256]{3,2,1,0:T(8,128)(2,1)}, u32[]{:S(2)}, u32[]{:S(2)}) async-start(bf16[32,2,16,256]{3,2,1,0:T(8,128)(2,1)} %shard_map.167), calls=%async_computation.1 | async-start | bytes 1048576 | tf_op jit(solution)/shard_map/all_to_all | solution.py:185
  13.4 10.3 %collective-permute-start.3 = (bf16[256,512]{1,0:T(8,128)(2,1)}, bf16[256,512]{1,0:T(8,128)(2,1)S(1)}, u32[]{:S(2)}, u32[]{:S(2)}) collective-permute-start(bf16[256,512]{1,0:T(8,128)(2,1)} %refs_0_.1), channel_id=1, source_target_pairs={{0,6},{1,7},{2,0},{3,1},{4,2},{5,3},{6,4},{7,5},{8,14},{9,15},{10,... | collective-permute-start | bytes 786440 | tf_op jit(solution)/shard_map/ppermute | solution.py:179
  13.5 23.5 %collective-permute-start.1 = (bf16[256,512]{1,0:T(8,128)(2,1)}, bf16[256,512]{1,0:T(8,128)(2,1)S(1)}, u32[]{:S(2)}, u32[]{:S(2)}) collective-permute-start(bf16[256,512]{1,0:T(8,128)(2,1)} %refs_0_.1), channel_id=1, source_target_pairs={{0,2},{1,3},{2,4},{3,5},{4,6},{5,7},{6,0},{7,1},{8,10},{9,11},{10,... | collective-permute-start | bytes 786440 | tf_op jit(solution)/shard_map/ppermute | solution.py:179
  17.6 28.7 %collective-permute-start.5 = (bf16[256,512]{1,0:T(8,128)(2,1)}, bf16[256,512]{1,0:T(8,128)(2,1)}, u32[]{:S(2)}, u32[]{:S(2)}) collective-permute-start(bf16[256,512]{1,0:T(8,128)(2,1)} %refs_0_.1), channel_id=1, source_target_pairs={{0,4},{1,5},{2,6},{3,7},{4,0},{5,1},{6,2},{7,3},{8,12},{9,13},{10,... | collective-permute-start | bytes 786440 | tf_op jit(solution)/shard_map/ppermute | solution.py:179
  22.1 24.9 %collective-permute-start = (bf16[256,512]{1,0:T(8,128)(2,1)}, bf16[256,512]{1,0:T(8,128)(2,1)S(1)}, u32[]{:S(2)}, u32[]{:S(2)}) collective-permute-start(bf16[256,512]{1,0:T(8,128)(2,1)} %refs_0_.1), channel_id=1, source_target_pairs={{0,1},{1,0},{2,3},{3,2},{4,5},{5,4},{6,7},{7,6},{8,9},{9,8},{10,11... | collective-permute-start | bytes 786440 | tf_op jit(solution)/shard_map/ppermute | solution.py:182
  23.7 23.4 %collective-permute-start.4 = (bf16[256,512]{1,0:T(8,128)(2,1)S(1)}, bf16[256,512]{1,0:T(8,128)(2,1)S(1)}, u32[]{:S(2)}, u32[]{:S(2)}) collective-permute-start(bf16[256,512]{1,0:T(8,128)(2,1)S(1)} %collective-permute-done.3.refs_4_), channel_id=1, source_target_pairs={{0,1},{1,0},{2,3},{3,2},{4,5},{5,4},{6,7},{7,6},{8,9},{9,8},{10,11... | collective-permute-start | bytes 786440 | tf_op jit(solution)/shard_map/ppermute | solution.py:182
  36.9 10.1 %collective-permute-start.2 = (bf16[256,512]{1,0:T(8,128)(2,1)S(1)}, bf16[256,512]{1,0:T(8,128)(2,1)S(1)}, u32[]{:S(2)}, u32[]{:S(2)}) collective-permute-start(bf16[256,512]{1,0:T(8,128)(2,1)S(1)} %collective-permute-done.1.refs_2_), channel_id=1, source_target_pairs={{0,1},{1,0},{2,3},{3,2},{4,5},{5,4},{6,7},{7,6},{8,9},{9,8},{10,11... | collective-permute-start | bytes 786440 | tf_op jit(solution)/shard_map/ppermute | solution.py:182
  36.9 14.3 %copy-start = (bf16[512,4096]{1,0:T(8,128)(2,1)S(1)}, bf16[512,4096]{1,0:T(8,128)(2,1)}, u32[]{:S(2)}) copy-start(bf16[512,4096]{1,0:T(8,128)(2,1)} %weight_pair.1) | copy-start | bytes 12582916
  46.3 4.9 %collective-permute-start.6 = (bf16[256,512]{1,0:T(8,128)(2,1)}, bf16[256,512]{1,0:T(8,128)(2,1)S(1)}, u32[]{:S(2)}, u32[]{:S(2)}) collective-permute-start(bf16[256,512]{1,0:T(8,128)(2,1)} %collective-permute-done.5.far), channel_id=1, source_target_pairs={{0,1},{1,0},{2,3},{3,2},{4,5},{5,4},{6,7},{7,6},{8,9},{9,8},{10,11... | collective-permute-start | bytes 786440 | tf_op jit(solution)/shard_map/ppermute | solution.py:182
  47.0 1.0 copy-start.16
  51.2 12.0 %copy-start.1 = (bf16[512,1024]{1,0:T(8,128)(2,1)S(1)}, bf16[512,1024]{1,0:T(8,128)(2,1)}, u32[]{:S(2)}) copy-start(bf16[512,1024]{1,0:T(8,128)(2,1)} %constant.36.clone.gather) | copy-start | bytes 3145732
  51.2 12.0 %copy-start.2 = (bf16[1024,512]{1,0:T(8,128)(2,1)S(1)}, bf16[1024,512]{1,0:T(8,128)(2,1)}, u32[]{:S(2)}) copy-start(bf16[1024,512]{1,0:T(8,128)(2,1)} %constant.35.clone.spread) | copy-start | bytes 3145732
  51.2 12.0 %copy-start.8 = (bf16[512,512]{1,0:T(8,128)(2,1)S(1)}, bf16[512,512]{1,0:T(8,128)(2,1)}, u32[]{:S(2)}) copy-start(bf16[512,512]{1,0:T(8,128)(2,1)} %constant.38.clone.back) | copy-start | bytes 1572868
  51.2 12.0 %copy-start.9 = (bf16[512,512]{1,0:T(8,128)(2,1)S(1)}, bf16[512,512]{1,0:T(8,128)(2,1)}, u32[]{:S(2)}) copy-start(bf16[512,512]{1,0:T(8,128)(2,1)} %constant.37.clone.ahead) | copy-start | bytes 1572868
  53.6 0.7 copy-start.18
  54.3 0.7 copy-start.19
  55.1 18.0 %all-to-all-start = ((bf16[32,16,256]{2,1,0:T(8,128)(2,1)}), bf16[32,16,256]{2,1,0:T(8,128)(2,1)S(1)}, u32[]{:S(2)}, u32[]{:S(2)}) async-start(bf16[32,16,256]{2,1,0:T(8,128)(2,1)} %copy-done.18), calls=%async_computation | async-start | bytes 524288 | tf_op jit(solution)/shard_map/all_to_all | solution.py:185
  63.3 1.0 copy-start.10
  64.2 0.9 copy-start.12
  70.3 0.7 copy-start.14
  73.0 1.0 copy-start.11
  74.0 0.9 copy-start.13
  74.9 0.9 copy-start.15
  75.9 25.0 %copy-start.4 = (bf16[256,512]{1,0:T(8,128)(2,1)S(1)}, bf16[256,512]{1,0:T(8,128)(2,1)}, u32[]{:S(2)}) copy-start(bf16[256,512]{1,0:T(8,128)(2,1)} %key.3) | copy-start | bytes 786436
  75.9 25.0 %copy-start.6 = (bf16[256,512]{1,0:T(8,128)(2,1)S(1)}, bf16[256,512]{1,0:T(8,128)(2,1)}, u32[]{:S(2)}) copy-start(bf16[256,512]{1,0:T(8,128)(2,1)} %value.3) | copy-start | bytes 786436
  75.9 25.0 %copy-start.20 = (bf16[256,512]{1,0:T(8,128)(2,1)S(1)}, bf16[256,512]{1,0:T(8,128)(2,1)}, u32[]{:S(2)}) copy-start(bf16[256,512]{1,0:T(8,128)(2,1)} %copy-done.19) | copy-start | bytes 786436

commit v2 on v1

v2 whole, which is shorter than its diff:
```python
import math

import jax
import jax.numpy as jnp
import ml_dtypes
import numpy as np
from jax import lax
from jax.experimental import pallas as pl
from jax.experimental.pallas import tpu as pltpu
from jax.sharding import PartitionSpec as P

BF = jnp.bfloat16
F32 = jnp.float32
PARTS = 32
ROWS = 256
CHANS = 16
TOKENS = PARTS * ROWS
HALF = CHANS // 2
WIDE = PARTS * HALF
SCALE = 1.0 / (math.sqrt(TOKENS) * TOKENS)


def tables():
    k1 = np.arange(PARTS)
    r = np.arange(ROWS)
    first = 2.0 * np.pi * (((4 * k1[:, None] + 1) * k1[None, :]) % (4 * PARTS)) / (4 * PARTS)
    twist = 2.0 * np.pi * (((4 * k1[:, None] + 1) * r[None, :]) % (4 * TOKENS)) / (4 * TOKENS)
    second = 2.0 * np.pi * ((r[:, None] * r[None, :]) % ROWS) / ROWS
    eye = np.eye(HALF)
    spread_re, spread_im = np.kron(np.cos(first), eye), np.kron(-np.sin(first), eye)
    gather = np.concatenate([spread_re.T, spread_im.T], 1)
    cos, sin = np.cos(second), np.sin(second)
    ahead = np.block([[cos, -sin], [sin, cos]])
    packed = np.concatenate([ahead, gather, np.concatenate([spread_re, spread_im], 1)], 0)
    wide = lambda a: np.broadcast_to(a[:, None, :], (PARTS, HALF, ROWS)).reshape(WIDE, ROWS)
    twists = np.stack([wide(np.cos(twist)), wide(np.sin(twist))])
    return packed.astype(ml_dtypes.bfloat16), twists.astype(np.float32)


def dot(a, b):
    return lax.dot_general(a, b, (((1,), (0,)), ((), ())), preferred_element_type=F32)


def dot_t(a, b):
    return lax.dot_general(a, b, (((1,), (1,)), ((), ())), preferred_element_type=F32)


def forward(signal, table, twists):
    re = dot(table[2 * ROWS + WIDE :, :WIDE], signal)
    im = dot(table[2 * ROWS + WIDE :, WIDE:], signal)
    cos, sin = twists[0], twists[1]
    turned = jnp.concatenate([(re * cos + im * sin).astype(BF), (im * cos - re * sin).astype(BF)], 1)
    out = dot(turned, table[: 2 * ROWS, :])
    return out[:, :ROWS], out[:, ROWS:]


def inverse(re, minus_im, table, twists):
    out = dot(jnp.concatenate([re.astype(BF), minus_im.astype(BF)], 1), table[: 2 * ROWS, :])
    re, minus_im = out[:, :ROWS], out[:, ROWS:]
    cos, sin = twists[0], twists[1]
    turned_re = (re * cos + minus_im * sin).astype(BF)
    turned_im = (re * sin - minus_im * cos).astype(BF)
    back = dot(table[2 * ROWS : 2 * ROWS + WIDE, :], jnp.concatenate([turned_re, turned_im], 0))
    return (back * SCALE).reshape(PARTS, HALF, ROWS)


def half_rows(block, half):
    rows = block.astype(F32).reshape(PARTS, 2, HALF, ROWS)[:, half]
    return rows.reshape(WIDE, ROWS).astype(BF)


def whole(halves):
    return jnp.stack(halves, 1).reshape(PARTS, CHANS, ROWS).astype(BF)


KEPT = 5


def early_kernel(source, table, twists, kept, got, sem):
    load = pltpu.make_async_copy(source, got, sem)
    load.start()
    load.wait()
    for half in range(2):
        xr, xi = forward(half_rows(got[:, 0], half), table, twists)
        hr, hi = forward(half_rows(got[:, 1], half), table, twists)
        conv = inverse(hr * xr - hi * xi, -(hr * xi + hi * xr), table, twists)
        for n, part in enumerate((xr, xi, hr, hi, conv.reshape(WIDE, ROWS))):
            kept[half * KEPT + n] = part


def late_kernel(got, kept, table, twists, out):
    results = []
    for half in range(2):
        gr, gi = forward(half_rows(got[...], half), table, twists)
        xr, xi, hr, hi, conv = (kept[half * KEPT + n] for n in range(KEPT))
        results.append((
            conv.reshape(PARTS, HALF, ROWS),
            inverse(hr * gr + hi * gi, hi * gr - hr * gi, table, twists),
            inverse(xr * gr + xi * gi, xi * gr - xr * gi, table, twists),
        ))
    for n in range(3):
        out[:, n] = whole([results[0][n], results[1][n]])


def columns(step, flip, width):
    holder = lax.axis_index("tp") ^ flip
    count = lax.axis_size("tp")
    way = 1 - 2 * lax.rem(holder, 2)
    owner = lax.rem(holder - 2 * step * way + count, count)
    return pl.ds(pl.multiple_of(owner * width, width), width)


def prepare_kernel(
    key, value, taps, own, weight, table, twists, pair,
    out, total, table_out, twists_out, k, v, t, o, w, sent, sems,
):
    width = own.shape[1]
    loads = [(key, k), (value, v), (taps, t), (own, o)]
    loads += [(weight.at[:, columns(0, flip, width)], w.at[flip]) for flip in range(2)]
    loads += [(table, table_out), (twists, twists_out)]
    loads = [pltpu.make_async_copy(*ends, sems.at[n]) for n, ends in enumerate(loads)]
    for load in loads:
        load.start()
    for load in loads[:2]:
        load.wait()
    inner = k[...].astype(F32) * v[...].astype(F32)
    sent[:, 0] = inner.T.astype(BF).reshape(PARTS, CHANS, ROWS)
    loads[2].wait()
    sent[:, 1] = t[...].T.astype(BF).reshape(PARTS, CHANS, ROWS)
    store = pltpu.make_async_copy(sent, out, sems.at[8])
    store.start()
    for load in loads[3:6]:
        load.wait()
    total[...] = dot_t(o[...], w[0]) + dot_t(pair[...], w[1])
    for load in loads[6:]:
        load.wait()
    store.wait()


def first_mix_kernel(weight, before, ahead, ahead_pair, behind, behind_pair, total, later, w, sems):
    width = ahead.shape[1]
    loads = []
    for n, (step, flip) in enumerate(((1, 0), (1, 1), (-1, 0), (-1, 1), (2, 0), (2, 1))):
        target = w.at[n] if n < 4 else later.at[n - 4]
        loads.append(
            pltpu.make_async_copy(weight.at[:, columns(step, flip, width)], target, sems.at[n])
        )
        loads[n].start()
    sums = before[...]
    for n, block in enumerate((ahead, ahead_pair, behind, behind_pair)):
        loads[n].wait()
        sums = sums + dot_t(block[...], w[n])
    total[...] = sums
    loads[4].wait()
    loads[5].wait()


def last_mix_kernel(weight, total, far, far_pair, gate, mix, out, mixed, sem):
    sums = total[...] + dot_t(far[...], weight[0]) + dot_t(far_pair[...], weight[1])
    mixed[...] = sums.astype(BF)
    store = pltpu.make_async_copy(mixed, mix, sem)
    store.start()
    grad = sums.astype(BF).astype(F32) * gate[...].astype(F32)
    out[...] = grad.T.astype(BF).reshape(PARTS, CHANS, ROWS)
    store.wait()


def finish_kernel(got, mix, key, value, *refs):
    outs, results, sems = refs[:4], refs[4:8], refs[8]

    def result(slot):
        return got[:, slot].reshape(PARTS * CHANS, ROWS).astype(F32).T

    def store(n):
        copy = pltpu.make_async_copy(results[n], outs[n], sems.at[n])
        copy.start()
        return copy

    results[3][...] = result(2)
    copies = [store(3)]
    inner = result(1)
    results[1][...] = (inner * value[...].astype(F32)).astype(BF)
    copies.append(store(1))
    results[2][...] = (inner * key[...].astype(F32)).astype(BF)
    copies.append(store(2))
    results[0][...] = (mix[...].astype(F32) * result(0)).astype(BF)
    copies.append(store(0))
    for copy in copies:
        copy.wait()


PARAMS = pltpu.CompilerParams(vmem_limit_bytes=40 * 1024 * 1024)


def call(kernel, outs, *args, spaces, scratch=(), flops=0):
    leaves = jax.tree.leaves(outs)
    nbytes = sum(a.size * a.dtype.itemsize for a in (*args, *leaves))
    spaces = [pltpu.HBM if letter == "h" else pltpu.VMEM for letter in spaces]
    specs = [pl.BlockSpec(memory_space=space) for space in spaces]
    args = [pltpu.with_memory_space_constraint(a, space) for a, space in zip(args, spaces)]
    placed = [space(a.shape, a.dtype) for a, space in zip(leaves, spaces[len(args) :])]
    results = pl.pallas_call(
        kernel,
        out_shape=placed,
        in_specs=specs[: len(args)],
        out_specs=specs[len(args) :],
        scratch_shapes=scratch,
        compiler_params=PARAMS,
        cost_estimate=pl.CostEstimate(flops=flops, bytes_accessed=nbytes, transcendentals=0),
    )(*args)
    return results if isinstance(outs, tuple) else results[0]


def shape(dims, dtype=BF):
    return jax.ShapeDtypeStruct(dims, dtype)


def shards(out_grad, gate_act, key_act, value_act, filter_taps, out_weight):
    count = lax.axis_size("tp")
    rows, chans = gate_act.shape

    def ring(block, way):
        hops = [(i, (i + way * (2 - 4 * (i % 2))) % count) for i in range(count)]
        return lax.ppermute(block, "tp", hops)

    def swap(block):
        return lax.ppermute(block, "tp", [(i, i ^ 1) for i in range(count)])

    def exchange(block):
        return lax.all_to_all(block, "ctx", split_axis=0, concat_axis=0, tiled=True)

    table, twists = (jnp.asarray(t) for t in tables())
    together = lax.optimization_barrier
    block = shape((PARTS, CHANS, ROWS))
    partial = shape((rows, chans), F32)
    held = pltpu.VMEM((rows, chans), BF)
    weights = lambda n: (n, chans, chans)
    sems = pltpu.SemaphoreType.DMA((14,))

    ahead = ring(out_grad, 1)
    pair = swap(out_grad)
    again, pair = together((out_grad, pair))
    behind = ring(again, -1)
    sent, total, table, twists = call(
        prepare_kernel,
        (shape((PARTS, 2, CHANS, ROWS)), partial, shape(table.shape), shape(twists.shape, F32)),
        key_act, value_act, filter_taps, out_grad, out_weight, table, twists, pair,
        spaces="hhhhhhhv" + "hvvv",
        scratch=[
            held, held, pltpu.VMEM((rows, chans), F32), held, pltpu.VMEM(weights(2), BF),
            pltpu.VMEM((PARTS, 2, CHANS, ROWS), BF), sems,
        ],
        flops=270_000_000,
    )
    got = exchange(sent)
    ahead, total = together((ahead, total))
    far = ring(ahead, 1)
    ahead, behind = together((ahead, behind))
    total, later = call(
        first_mix_kernel, (partial, shape(weights(2))),
        out_weight, total, ahead, swap(ahead), behind, swap(behind),
        spaces="hvvvvv" + "vv",
        scratch=[pltpu.VMEM(weights(4), BF), sems], flops=7_000_000_000,
    )
    kept = call(
        early_kernel, shape((2 * KEPT, WIDE, ROWS), F32), got, table, twists,
        spaces="hvv" + "v",
        scratch=[pltpu.VMEM((PARTS, 2, CHANS, ROWS), BF), pltpu.SemaphoreType.DMA],
        flops=1_200_000_000,
    )
    far, total, kept = together((far, total, kept))
    mix, sent = call(
        last_mix_kernel, (shape((rows, chans)), block),
        later, total, far, swap(far), gate_act,
        spaces="vvvvv" + "hv",
        scratch=[held, pltpu.SemaphoreType.DMA], flops=300_000_000_000,
    )
    got = exchange(sent)
    sent = call(
        late_kernel, shape((PARTS, 3, CHANS, ROWS)), got, kept, table, twists,
        spaces="vvvv" + "v", flops=1_200_000_000,
    )
    got = exchange(sent)
    return tuple(call(
        finish_kernel,
        (shape((rows, chans)), shape((rows, chans)), shape((rows, chans)), shape((rows, chans), F32)),
        got, mix, key_act, value_act,
        spaces="vvvv" + "hhhh",
        scratch=[held, held, held, pltpu.VMEM((rows, chans), F32), pltpu.SemaphoreType.DMA((4,))],
    ))


def solution(mesh):
    in_specs = (
        P("ctx", "tp"),
        P("ctx", "tp"),
        P("ctx", "tp"),
        P("ctx", "tp"),
        P("ctx", "tp"),
        P("tp", None),
    )
    out_specs = (P("ctx", "tp"), P("ctx", "tp"), P("ctx", "tp"), P("ctx", "tp"))
    return jax.shard_map(shards, mesh=mesh, in_specs=in_specs, out_specs=out_specs, check_vma=False)
```

time: 103 us -> 73 us (0.71)
  the two profiles are of different devices: /device:TPU:64 before, /device:TPU:32 now
where the time goes in v2:
time: 73 us; the launch traced here: 72.7 us
  blocking collectives  33.6 us (46%)
  starting transfers between devices  17.1 us (23%)
  Pallas kernels  12.7 us (17%)
  waiting for transfers between devices  7.5 us (10%)
  local copies, waits for them, and re-layouts  1.01 us (1%)
  between operations  0.76 us (1%)
    all_to_all x2, blocking collectives, exchange(): return lax.all_to_all(block, 'ctx', split_axis=0, concat_axis=0, tiled=True)  33.6 us
    pallas_call x6, Pallas kernels, call(): pl.pallas_call(kernel, out_shape=placed, in_specs=specs[:len(args)], out_...  12.7 us
    all_to_all x1, starting transfers between devices, exchange(): return lax.all_to_all(block, 'ctx', split_axis=0, concat_axis=0, tiled=True)  8.62 us
    ppermute x3, starting transfers between devices, ring(): return lax.ppermute(block, 'tp', hops)  7.74 us
    all_to_all x1, waiting for transfers between devices, exchange(): return lax.all_to_all(block, 'ctx', split_axis=0, concat_axis=0, tiled=True)  5.18 us
    ppermute x4, waiting for transfers between devices, swap(): return lax.ppermute(block, 'tp', [(i, i ^ 1) for i in range(count)])  2.32 us
  transfers between devices with their start and end apart: 8, of which 4 were waited for; matrix products, arithmetic and copies ran while one was open for 0% of the time, Pallas kernels for 11%

profile of v2, /device:TPU:32, one launch (start us, length us, event | category | flops | bytes accessed | tf_op | source)
XLA Modules:
  0.0 72.7 jit_solution(6237762691810488707)
XLA Ops:
  0.6 0.1 collective-permute-start.1
  0.7 3.3 %collective-permute-start = (bf16[256,512]{1,0:T(8,128)(2,1)}, bf16[256,512]{1,0:T(8,128)(2,1)S(1)}, u32[]{:S(2)}, u32[]{:S(2)}) collective-permute-start(bf16[256,512]{1,0:T(8,128)(2,1)} %own.1), channel_id=1, source_target_pairs={{0,2},{1,7},{2,4},{3,1},{4,6},{5,3},{6,0},{7,5},{8,10},{9,15},{10,... | collective-permute-start | bytes 786440 | tf_op jit(solution)/shard_map/ppermute | solution.py:224
  4.1 0.0 collective-permute-done.1.pair
  4.1 3.8 %collective-permute-start.2 = (bf16[256,512]{1,0:T(8,128)(2,1)}, bf16[256,512]{1,0:T(8,128)(2,1)S(1)}, u32[]{:S(2)}, u32[]{:S(2)}) collective-permute-start(bf16[256,512]{1,0:T(8,128)(2,1)} %own.1), channel_id=1, source_target_pairs={{0,6},{1,3},{2,0},{3,5},{4,2},{5,7},{6,4},{7,1},{8,14},{9,11},{10,... | collective-permute-start | bytes 786440 | tf_op jit(solution)/shard_map/ppermute | solution.py:224
  7.9 2.3 %shard_map.111 = (bf16[32,2,16,256]{3,2,1,0:T(8,128)(2,1)}, f32[256,512]{1,0:T(8,128)S(1)}, bf16[1024,512]{1,0:T(8,128)(2,1)S(1)}, f32[2,256,256]{2,1,0:T(8,128)S(1)}) custom-call(bf16[256,512]{1,0:T(8,128)(2,1)} %key.3, bf16[256,512]{1,0:T(8,128)(2,1)} %value.3, f32[256,512]{1,0:T(8,128)} %taps.1, bf16[256,512]{1,0:T(8,128)(2,1)} %own.1, ...), custom_call_target="tpu_custom_call" | custom-call | flops 270000000 | bytes 9961472 | tf_op jit(solution)/shard_map/pallas_call | solution.py:202
  10.1 8.6 %all-to-all-start = ((bf16[32,2,16,256]{3,2,1,0:T(8,128)(2,1)}), bf16[32,2,16,256]{3,2,1,0:T(8,128)(2,1)}, u32[]{:S(2)}, u32[]{:S(2)}) async-start(bf16[32,2,16,256]{3,2,1,0:T(8,128)(2,1)} %get-tuple-element.30), calls=%async_computation | async-start | bytes 1048576 | tf_op jit(solution)/shard_map/all_to_all | solution.py:230
  18.8 0.0 collective-permute-done.ahead
  18.8 0.0 collective-permute-done.2.behind
  18.8 0.3 collective-permute-start.3
  19.1 0.3 collective-permute-start.4
  19.4 0.6 collective-permute-start.5
  20.0 0.4 collective-permute-done.3.ahead_pair
  20.4 0.4 collective-permute-done.4.behind_pair
  20.8 2.2 %shard_map.112 = (f32[256,512]{1,0:T(8,128)S(1)}, bf16[2,512,512]{2,1,0:T(8,128)(2,1)S(1)}) custom-call(bf16[512,4096]{1,0:T(8,128)(2,1)} %weight.3, f32[256,512]{1,0:T(8,128)S(1)} %get-tuple-element.23.before, bf16[256,512]{1,0:T(8,128)(2,1)S(1)} %collective-permute-done.ahead, bf16[256,512]{1,0:T(8,128)(2,1)S(1)} %collective-permute-done.3.ahead_pair, ...), custom_call_target="tpu_custom_call" | custom-call | flops 7000000000 | bytes 7340032 | tf_op jit(solution)/shard_map/pallas_call | solution.py:202
  23.0 0.0 copy-start.4
  23.0 1.0 %copy-done.4 = bf16[2,512,512]{2,1,0:T(8,128)(2,1)} copy-done((bf16[2,512,512]{2,1,0:T(8,128)(2,1)}, bf16[2,512,512]{2,1,0:T(8,128)(2,1)S(1)}, u32[]{:S(2)}) %copy-start.4) | copy-done | bytes 1048600
  23.9 0.0 copy-start.3
  23.9 5.2 %all-to-all-done.source = bf16[32,2,16,256]{3,2,1,0:T(8,128)(2,1)} async-done(((bf16[32,2,16,256]{3,2,1,0:T(8,128)(2,1)}), bf16[32,2,16,256]{3,2,1,0:T(8,128)(2,1)}, u32[]{:S(2)}, u32[]{:S(2)}) %all-to-all-start) | async-done | bytes 524320 | tf_op jit(solution)/shard_map/all_to_all | solution.py:230
  29.1 0.0 copy-start.5
  29.1 3.3 %shard_map.113.kept = f32[10,256,256]{2,1,0:T(8,128)S(1)} custom-call(bf16[32,2,16,256]{3,2,1,0:T(8,128)(2,1)} %all-to-all-done.source, bf16[1024,512]{1,0:T(8,128)(2,1)S(1)} %get-tuple-element.31.table, f32[2,256,256]{2,1,0:T(8,128)S(1)} %get-tuple-element.32.twists), custom_call_target="tpu_custom_call" | custom-call | flops 1200000000 | bytes 4718592 | tf_op jit(solution)/shard_map/pallas_call | solution.py:202
  32.4 0.0 collective-permute-done.5.far
  32.4 0.1 collective-permute-start.6
  32.5 1.5 %collective-permute-done.6.far_pair = bf16[256,512]{1,0:T(8,128)(2,1)S(1)} collective-permute-done((bf16[256,512]{1,0:T(8,128)(2,1)S(1)}, bf16[256,512]{1,0:T(8,128)(2,1)S(1)}, u32[]{:S(2)}, u32[]{:S(2)}) %collective-permute-start.6) | collective-permute-done | bytes 262176 | tf_op jit(solution)/shard_map/ppermute | solution.py:227
  34.1 0.0 copy-done.3
  34.1 0.0 copy-done.5
  34.1 1.2 %shard_map.114 = (bf16[256,512]{1,0:T(8,128)(2,1)}, bf16[32,16,256]{2,1,0:T(8,128)(2,1)S(1)}) custom-call(bf16[2,512,512]{2,1,0:T(8,128)(2,1)S(1)} %copy-done.5, f32[256,512]{1,0:T(8,128)S(1)} %get-tuple-element.33.total, bf16[256,512]{1,0:T(8,128)(2,1)S(1)} %collective-permute-done.5.far, bf16[256,512]{1,0:T(8,128)(2,1)S(1)} %collective-permute-done.6.far_pair, ...), custom_call_target="tpu_custom_call" | custom-call | flops 299999985664 | bytes 2883584 | tf_op jit(solution)/shard_map/pallas_call | solution.py:202
  35.3 0.0 copy-start
  35.3 0.0 copy-start.1
  35.3 0.0 copy-start.2
  35.3 16.2 %all_to_all.15.got = bf16[32,16,256]{2,1,0:T(8,128)(2,1)S(1)} all-to-all(bf16[32,16,256]{2,1,0:T(8,128)(2,1)S(1)} %get-tuple-element.35), channel_id=1, replica_groups=mesh['ctx'=32,'tp'=8] {'ctx'}, dimensions={0} | all-to-all | bytes 524288 | tf_op jit(solution)/shard_map/all_to_all | solution.py:230
  51.6 2.5 %shard_map.115 = bf16[32,3,16,256]{3,2,1,0:T(8,128)(2,1)S(1)} custom-call(bf16[32,16,256]{2,1,0:T(8,128)(2,1)S(1)} %all_to_all.15.got, f32[10,256,256]{2,1,0:T(8,128)S(1)} %shard_map.113.kept, bf16[1024,512]{1,0:T(8,128)(2,1)S(1)} %get-tuple-element.31.table, f32[2,256,256]{2,1,0:T(8,128)S(1)} %get-tuple-element.32.twists), custom_call_target="tpu_custom_call" | custom-call | flops 1200000000 | bytes 5242880 | tf_op jit(solution)/shard_map/pallas_call | solution.py:202
  54.1 17.4 %all_to_all.16.got = bf16[32,3,16,256]{3,2,1,0:T(8,128)(2,1)S(1)} all-to-all(bf16[32,3,16,256]{3,2,1,0:T(8,128)(2,1)S(1)} %shard_map.115), channel_id=1, replica_groups=mesh['ctx'=32,'tp'=8] {'ctx'}, dimensions={0} | all-to-all | bytes 1572864 | tf_op jit(solution)/shard_map/all_to_all | solution.py:230
  71.5 0.0 copy-done
  71.5 0.0 copy-done.1
  71.5 0.0 copy-done.2
  71.5 1.2 %shard_map.116 = (bf16[256,512]{1,0:T(8,128)(2,1)}, bf16[256,512]{1,0:T(8,128)(2,1)}, bf16[256,512]{1,0:T(8,128)(2,1)}, f32[256,512]{1,0:T(8,128)}) custom-call(bf16[32,3,16,256]{3,2,1,0:T(8,128)(2,1)S(1)} %all_to_all.16.got, bf16[256,512]{1,0:T(8,128)(2,1)S(1)} %copy-done.2, bf16[256,512]{1,0:T(8,128)(2,1)S(1)} %copy-done, bf16[256,512]{1,0:T(8,128)(2,1)S(1)} %copy-done.1), custom_call_target="tpu_custom_call" | custom-call | bytes 2883584 | tf_op jit(solution)/shard_map/pallas_call | solution.py:202
Async XLA Ops:
  0.6 3.5 %collective-permute-start.1 = (bf16[256,512]{1,0:T(8,128)(2,1)}, bf16[256,512]{1,0:T(8,128)(2,1)S(1)}, u32[]{:S(2)}, u32[]{:S(2)}) collective-permute-start(bf16[256,512]{1,0:T(8,128)(2,1)} %own.1), channel_id=1, source_target_pairs={{0,1},{1,0},{2,3},{3,2},{4,5},{5,4},{6,7},{7,6},{8,9},{9,8},{10,11... | collective-permute-start | bytes 786440 | tf_op jit(solution)/shard_map/ppermute | solution.py:227
  0.7 18.0 %collective-permute-start = (bf16[256,512]{1,0:T(8,128)(2,1)}, bf16[256,512]{1,0:T(8,128)(2,1)S(1)}, u32[]{:S(2)}, u32[]{:S(2)}) collective-permute-start(bf16[256,512]{1,0:T(8,128)(2,1)} %own.1), channel_id=1, source_target_pairs={{0,2},{1,7},{2,4},{3,1},{4,6},{5,3},{6,0},{7,5},{8,10},{9,15},{10,... | collective-permute-start | bytes 786440 | tf_op jit(solution)/shard_map/ppermute | solution.py:224
  4.1 14.7 %collective-permute-start.2 = (bf16[256,512]{1,0:T(8,128)(2,1)}, bf16[256,512]{1,0:T(8,128)(2,1)S(1)}, u32[]{:S(2)}, u32[]{:S(2)}) collective-permute-start(bf16[256,512]{1,0:T(8,128)(2,1)} %own.1), channel_id=1, source_target_pairs={{0,6},{1,3},{2,0},{3,5},{4,2},{5,7},{6,4},{7,1},{8,14},{9,11},{10,... | collective-permute-start | bytes 786440 | tf_op jit(solution)/shard_map/ppermute | solution.py:224
  10.1 19.0 %all-to-all-start = ((bf16[32,2,16,256]{3,2,1,0:T(8,128)(2,1)}), bf16[32,2,16,256]{3,2,1,0:T(8,128)(2,1)}, u32[]{:S(2)}, u32[]{:S(2)}) async-start(bf16[32,2,16,256]{3,2,1,0:T(8,128)(2,1)} %get-tuple-element.30), calls=%async_computation | async-start | bytes 1048576 | tf_op jit(solution)/shard_map/all_to_all | solution.py:230
  18.8 1.6 %collective-permute-start.3 = (bf16[256,512]{1,0:T(8,128)(2,1)S(1)}, bf16[256,512]{1,0:T(8,128)(2,1)S(1)}, u32[]{:S(2)}, u32[]{:S(2)}) collective-permute-start(bf16[256,512]{1,0:T(8,128)(2,1)S(1)} %collective-permute-done.ahead), channel_id=1, source_target_pairs={{0,1},{1,0},{2,3},{3,2},{4,5},{5,4},{6,7},{7,6},{8,9},{9,8},{10,11... | collective-permute-start | bytes 786440 | tf_op jit(solution)/shard_map/ppermute | solution.py:227
  19.1 1.7 %collective-permute-start.4 = (bf16[256,512]{1,0:T(8,128)(2,1)S(1)}, bf16[256,512]{1,0:T(8,128)(2,1)S(1)}, u32[]{:S(2)}, u32[]{:S(2)}) collective-permute-start(bf16[256,512]{1,0:T(8,128)(2,1)S(1)} %collective-permute-done.2.behind), channel_id=1, source_target_pairs={{0,1},{1,0},{2,3},{3,2},{4,5},{5,4},{6,7},{7,6},{8,9},{9,8},{10,11... | collective-permute-start | bytes 786440 | tf_op jit(solution)/shard_map/ppermute | solution.py:227
  19.4 13.1 %collective-permute-start.5 = (bf16[256,512]{1,0:T(8,128)(2,1)S(1)}, bf16[256,512]{1,0:T(8,128)(2,1)S(1)}, u32[]{:S(2)}, u32[]{:S(2)}) collective-permute-start(bf16[256,512]{1,0:T(8,128)(2,1)S(1)} %collective-permute-done.ahead), channel_id=1, source_target_pairs={{0,2},{1,7},{2,4},{3,1},{4,6},{5,3},{6,0},{7,5},{8,10},{9,15},{10,... | collective-permute-start | bytes 786440 | tf_op jit(solution)/shard_map/ppermute | solution.py:224
  23.0 1.0 %copy-start.4 = (bf16[2,512,512]{2,1,0:T(8,128)(2,1)}, bf16[2,512,512]{2,1,0:T(8,128)(2,1)S(1)}, u32[]{:S(2)}) copy-start(bf16[2,512,512]{2,1,0:T(8,128)(2,1)S(1)} %get-tuple-element.28.weight) | copy-start | bytes 3145732
  23.9 10.1 %copy-start.3 = (bf16[256,512]{1,0:T(8,128)(2,1)S(1)}, bf16[256,512]{1,0:T(8,128)(2,1)}, u32[]{:S(2)}) copy-start(bf16[256,512]{1,0:T(8,128)(2,1)} %gate.1) | copy-start | bytes 786436
  29.1 4.9 %copy-start.5 = (bf16[2,512,512]{2,1,0:T(8,128)(2,1)S(1)}, bf16[2,512,512]{2,1,0:T(8,128)(2,1)}, u32[]{:S(2)}) copy-start(bf16[2,512,512]{2,1,0:T(8,128)(2,1)} %copy-done.4) | copy-start | bytes 3145732
  32.4 1.6 %collective-permute-start.6 = (bf16[256,512]{1,0:T(8,128)(2,1)S(1)}, bf16[256,512]{1,0:T(8,128)(2,1)S(1)}, u32[]{:S(2)}, u32[]{:S(2)}) collective-permute-start(bf16[256,512]{1,0:T(8,128)(2,1)S(1)} %collective-permute-done.5.far), channel_id=1, source_target_pairs={{0,1},{1,0},{2,3},{3,2},{4,5},{5,4},{6,7},{7,6},{8,9},{9,8},{10,11... | collective-permute-start | bytes 786440 | tf_op jit(solution)/shard_map/ppermute | solution.py:227
  35.3 36.2 %copy-start = (bf16[256,512]{1,0:T(8,128)(2,1)S(1)}, bf16[256,512]{1,0:T(8,128)(2,1)}, u32[]{:S(2)}) copy-start(bf16[256,512]{1,0:T(8,128)(2,1)} %key.3) | copy-start | bytes 786436
  35.3 36.2 %copy-start.1 = (bf16[256,512]{1,0:T(8,128)(2,1)S(1)}, bf16[256,512]{1,0:T(8,128)(2,1)}, u32[]{:S(2)}) copy-start(bf16[256,512]{1,0:T(8,128)(2,1)} %value.3) | copy-start | bytes 786436
  35.3 36.2 %copy-start.2 = (bf16[256,512]{1,0:T(8,128)(2,1)S(1)}, bf16[256,512]{1,0:T(8,128)(2,1)}, u32[]{:S(2)}) copy-start(bf16[256,512]{1,0:T(8,128)(2,1)} %get-tuple-element.37.mix) | copy-start | bytes 786436

commit v3 on v2

--- a/solution.py
+++ b/solution.py
@@ -45,61 +45,71 @@
     return lax.dot_general(a, b, (((1,), (1,)), ((), ())), preferred_element_type=F32)
 
 
-def forward(signal, table, twists):
-    re = dot(table[2 * ROWS + WIDE :, :WIDE], signal)
-    im = dot(table[2 * ROWS + WIDE :, WIDE:], signal)
+def spectra(signals, table, twists):
     cos, sin = twists[0], twists[1]
-    turned = jnp.concatenate([(re * cos + im * sin).astype(BF), (im * cos - re * sin).astype(BF)], 1)
-    out = dot(turned, table[: 2 * ROWS, :])
-    return out[:, :ROWS], out[:, ROWS:]
-
-
-def inverse(re, minus_im, table, twists):
-    out = dot(jnp.concatenate([re.astype(BF), minus_im.astype(BF)], 1), table[: 2 * ROWS, :])
-    re, minus_im = out[:, :ROWS], out[:, ROWS:]
+    turned = []
+    for signal in signals:
+        re = dot(table[2 * ROWS + WIDE :, :WIDE], signal)
+        im = dot(table[2 * ROWS + WIDE :, WIDE:], signal)
+        turned.append(
+            jnp.concatenate([(re * cos + im * sin).astype(BF), (im * cos - re * sin).astype(BF)], 1)
+        )
+    return dot(jnp.concatenate(turned, 0), table[: 2 * ROWS, :])
+
+
+def inverses(pairs, table, twists):
+    rows = [jnp.concatenate([re.astype(BF), minus_im.astype(BF)], 1) for re, minus_im in pairs]
+    out = dot(jnp.concatenate(rows, 0), table[: 2 * ROWS, :])
     cos, sin = twists[0], twists[1]
-    turned_re = (re * cos + minus_im * sin).astype(BF)
-    turned_im = (re * sin - minus_im * cos).astype(BF)
-    back = dot(table[2 * ROWS : 2 * ROWS + WIDE, :], jnp.concatenate([turned_re, turned_im], 0))
-    return (back * SCALE).reshape(PARTS, HALF, ROWS)
-
-
-def half_rows(block, half):
-    rows = block.astype(F32).reshape(PARTS, 2, HALF, ROWS)[:, half]
-    return rows.reshape(WIDE, ROWS).astype(BF)
-
-
-def whole(halves):
-    return jnp.stack(halves, 1).reshape(PARTS, CHANS, ROWS).astype(BF)
+    results = []
+    for n in range(len(pairs)):
+        re = out[n * WIDE : (n + 1) * WIDE, :ROWS]
+        minus_im = out[n * WIDE : (n + 1) * WIDE, ROWS:]
+        turned_re = (re * cos + minus_im * sin).astype(BF)
+        turned_im = (re * sin - minus_im * cos).astype(BF)
+        back = dot(table[2 * ROWS : 2 * ROWS + WIDE, :], jnp.concatenate([turned_re, turned_im], 0))
+        results.append((back * SCALE).reshape(PARTS, HALF, ROWS))
+    return results
+
+
+def halves(block):
+    rows = block.astype(F32).reshape(PARTS, 2, HALF, ROWS)
+    return [rows[:, half].reshape(WIDE, ROWS).astype(BF) for half in range(2)]
+
+
+def whole(parts):
+    return jnp.stack(parts, 1).reshape(PARTS, CHANS, ROWS).astype(BF)
 
 
 KEPT = 5
 
 
-def early_kernel(source, table, twists, kept, got, sem):
-    load = pltpu.make_async_copy(source, got, sem)
-    load.start()
-    load.wait()
+def early_kernel(got, table, twists, kept):
+    out = spectra(halves(got[:, 0]) + halves(got[:, 1]), table, twists)
+    pairs = []
     for half in range(2):
-        xr, xi = forward(half_rows(got[:, 0], half), table, twists)
-        hr, hi = forward(half_rows(got[:, 1], half), table, twists)
-        conv = inverse(hr * xr - hi * xi, -(hr * xi + hi * xr), table, twists)
-        for n, part in enumerate((xr, xi, hr, hi, conv.reshape(WIDE, ROWS))):
+        x, h = out[half * WIDE : (half + 1) * WIDE], out[(half + 2) * WIDE : (half + 3) * WIDE]
+        xr, xi, hr, hi = x[:, :ROWS], x[:, ROWS:], h[:, :ROWS], h[:, ROWS:]
+        for n, part in enumerate((xr, xi, hr, hi)):
             kept[half * KEPT + n] = part
+        pairs.append((hr * xr - hi * xi, -(hr * xi + hi * xr)))
+    for half, conv in enumerate(inverses(pairs, table, twists)):
+        kept[half * KEPT + 4] = conv.reshape(WIDE, ROWS)
 
 
 def late_kernel(got, kept, table, twists, out):
-    results = []
+    out[:, 0] = whole([kept[half * KEPT + 4].reshape(PARTS, HALF, ROWS) for half in range(2)])
+    grad = spectra(halves(got[...]), table, twists)
+    pairs = []
     for half in range(2):
-        gr, gi = forward(half_rows(got[...], half), table, twists)
-        xr, xi, hr, hi, conv = (kept[half * KEPT + n] for n in range(KEPT))
-        results.append((
-            conv.reshape(PARTS, HALF, ROWS),
-            inverse(hr * gr + hi * gi, hi * gr - hr * gi, table, twists),
-            inverse(xr * gr + xi * gi, xi * gr - xr * gi, table, twists),
-        ))
-    for n in range(3):
-        out[:, n] = whole([results[0][n], results[1][n]])
+        g = grad[half * WIDE : (half + 1) * WIDE]
+        gr, gi = g[:, :ROWS], g[:, ROWS:]
+        xr, xi, hr, hi = (kept[half * KEPT + n] for n in range(4))
+        pairs.append((hr * gr + hi * gi, hi * gr - hr * gi))
+        pairs.append((xr * gr + xi * gi, xi * gr - xr * gi))
+    results = inverses(pairs, table, twists)
+    out[:, 1] = whole([results[0], results[2]])
+    out[:, 2] = whole([results[1], results[3]])
 
 
 def columns(step, flip, width):
@@ -264,8 +274,7 @@
     )
     kept = call(
         early_kernel, shape((2 * KEPT, WIDE, ROWS), F32), got, table, twists,
-        spaces="hvv" + "v",
-        scratch=[pltpu.VMEM((PARTS, 2, CHANS, ROWS), BF), pltpu.SemaphoreType.DMA],
+        spaces="vvv" + "v",
         flops=1_200_000_000,
     )
     far, total, kept = together((far, total, kept))

time: 73 us -> 71.7 us (0.982)
  Pallas kernels: 12.7 us -> 9.99 us
  blocking collectives: 33.6 us -> 34.9 us
  waiting for transfers between devices: 7.5 us -> 6.22 us
  local copies, waits for them, and re-layouts: 1.01 us -> 1.82 us
    pallas_call x6, Pallas kernels: 12.7 us -> 9.99 us  [call(): pl.pallas_call(kernel, out_shape=placed, in_specs=specs[:len(args)], out_...]
    all_to_all x2, blocking collectives: 33.6 us -> 34.9 us  [exchange(): return lax.all_to_all(block, 'ctx', split_axis=0, concat_axis=0, tiled=True)]
    all_to_all x1, waiting for transfers between devices: 5.18 us -> 4.32 us  [exchange(): return lax.all_to_all(block, 'ctx', split_axis=0, concat_axis=0, tiled=True)]
    unnamed x12 -> x16, local copies, waits for them, and re-layouts: 1.01 us -> 1.82 us
  transfers between devices with their start and end apart: 8 -> 8, of which waited for: 4 -> 4; matrix products, arithmetic and copies ran while one was open for 0% -> 0% of each run, Pallas kernels for 11% -> 8%
where the time goes in v3:
time: 71.7 us; the launch traced here: 71.4 us
  blocking collectives  34.9 us (49%)
  starting transfers between devices  17.7 us (25%)
  Pallas kernels  9.99 us (14%)
  waiting for transfers between devices  6.22 us (9%)
  local copies, waits for them, and re-layouts  1.82 us (3%)
  between operations  0.76 us (1%)
    all_to_all x2, blocking collectives, exchange(): return lax.all_to_all(block, 'ctx', split_axis=0, concat_axis=0, tiled=True)  34.9 us
    pallas_call x6, Pallas kernels, call(): pl.pallas_call(kernel, out_shape=placed, in_specs=specs[:len(args)], out_...  9.99 us
    all_to_all x1, starting transfers between devices, exchange(): return lax.all_to_all(block, 'ctx', split_axis=0, concat_axis=0, tiled=True)  8.56 us
    ppermute x3, starting transfers between devices, ring(): return lax.ppermute(block, 'tp', hops)  7.79 us
    all_to_all x1, waiting for transfers between devices, exchange(): return lax.all_to_all(block, 'ctx', split_axis=0, concat_axis=0, tiled=True)  4.32 us
    ppermute x4, waiting for transfers between devices, swap(): return lax.ppermute(block, 'tp', [(i, i ^ 1) for i in range(count)])  1.9 us
    unnamed x16, local copies, waits for them, and re-layouts  1.82 us
  transfers between devices with their start and end apart: 8, of which 4 were waited for; matrix products, arithmetic and copies ran while one was open for 0% of the time, Pallas kernels for 8%

profile of v3, /device:TPU:32, one launch (start us, length us, event | category | flops | bytes accessed | tf_op | source)
XLA Modules:
  0.0 71.4 jit_solution(9040397798194358817)
XLA Ops:
  0.6 0.1 collective-permute-start.1
  0.7 3.3 %collective-permute-start = (bf16[256,512]{1,0:T(8,128)(2,1)}, bf16[256,512]{1,0:T(8,128)(2,1)S(1)}, u32[]{:S(2)}, u32[]{:S(2)}) collective-permute-start(bf16[256,512]{1,0:T(8,128)(2,1)} %own.1), channel_id=1, source_target_pairs={{0,2},{1,7},{2,4},{3,1},{4,6},{5,3},{6,0},{7,5},{8,10},{9,15},{10,... | collective-permute-start | bytes 786440 | tf_op jit(solution)/shard_map/ppermute | solution.py:234
  4.1 0.0 collective-permute-done.1.pair
  4.1 3.8 %collective-permute-start.2 = (bf16[256,512]{1,0:T(8,128)(2,1)}, bf16[256,512]{1,0:T(8,128)(2,1)S(1)}, u32[]{:S(2)}, u32[]{:S(2)}) collective-permute-start(bf16[256,512]{1,0:T(8,128)(2,1)} %own.1), channel_id=1, source_target_pairs={{0,6},{1,3},{2,0},{3,5},{4,2},{5,7},{6,4},{7,1},{8,14},{9,11},{10,... | collective-permute-start | bytes 786440 | tf_op jit(solution)/shard_map/ppermute | solution.py:234
  7.9 2.3 %shard_map.111 = (bf16[32,2,16,256]{3,2,1,0:T(8,128)(2,1)}, f32[256,512]{1,0:T(8,128)S(1)}, bf16[1024,512]{1,0:T(8,128)(2,1)S(1)}, f32[2,256,256]{2,1,0:T(8,128)S(1)}) custom-call(bf16[256,512]{1,0:T(8,128)(2,1)} %key.3, bf16[256,512]{1,0:T(8,128)(2,1)} %value.3, f32[256,512]{1,0:T(8,128)} %taps.1, bf16[256,512]{1,0:T(8,128)(2,1)} %own.1, ...), custom_call_target="tpu_custom_call" | custom-call | flops 270000000 | bytes 9961472 | tf_op jit(solution)/shard_map/pallas_call | solution.py:212
  10.1 8.6 %all-to-all-start = ((bf16[32,2,16,256]{3,2,1,0:T(8,128)(2,1)}), bf16[32,2,16,256]{3,2,1,0:T(8,128)(2,1)S(1)}, u32[]{:S(2)}, u32[]{:S(2)}) async-start(bf16[32,2,16,256]{3,2,1,0:T(8,128)(2,1)} %get-tuple-element.30), calls=%async_computation | async-start | bytes 1048576 | tf_op jit(solution)/shard_map/all_to_all | solution.py:240
  18.7 0.0 collective-permute-done.ahead
  18.7 0.0 collective-permute-done.2.behind
  18.7 0.4 collective-permute-start.3
  19.1 0.2 collective-permute-start.4
  19.3 0.7 collective-permute-start.5
  20.0 0.4 collective-permute-done.3.ahead_pair
  20.3 0.4 collective-permute-done.4.behind_pair
  20.7 2.2 %shard_map.112 = (f32[256,512]{1,0:T(8,128)S(1)}, bf16[2,512,512]{2,1,0:T(8,128)(2,1)S(1)}) custom-call(bf16[512,4096]{1,0:T(8,128)(2,1)} %weight.3, f32[256,512]{1,0:T(8,128)S(1)} %get-tuple-element.23.before, bf16[256,512]{1,0:T(8,128)(2,1)S(1)} %collective-permute-done.ahead, bf16[256,512]{1,0:T(8,128)(2,1)S(1)} %collective-permute-done.3.ahead_pair, ...), custom_call_target="tpu_custom_call" | custom-call | flops 7000000000 | bytes 7340032 | tf_op jit(solution)/shard_map/pallas_call | solution.py:212
  22.9 0.0 copy-start.4
  22.9 1.0 %copy-done.4 = bf16[2,512,512]{2,1,0:T(8,128)(2,1)} copy-done((bf16[2,512,512]{2,1,0:T(8,128)(2,1)}, bf16[2,512,512]{2,1,0:T(8,128)(2,1)S(1)}, u32[]{:S(2)}) %copy-start.4) | copy-done | bytes 1048600
  23.9 0.0 copy-start.6
  23.9 0.8 %copy-done.6 = f32[256,512]{1,0:T(8,128)} copy-done((f32[256,512]{1,0:T(8,128)}, f32[256,512]{1,0:T(8,128)S(1)}, u32[]{:S(2)}) %copy-start.6) | copy-done | bytes 524312
  24.7 0.0 copy-start.3
  24.7 4.3 %all-to-all-done.got = bf16[32,2,16,256]{3,2,1,0:T(8,128)(2,1)S(1)} async-done(((bf16[32,2,16,256]{3,2,1,0:T(8,128)(2,1)}), bf16[32,2,16,256]{3,2,1,0:T(8,128)(2,1)S(1)}, u32[]{:S(2)}, u32[]{:S(2)}) %all-to-all-start) | async-done | bytes 524320 | tf_op jit(solution)/shard_map/all_to_all | solution.py:240
  29.0 0.0 copy-start.5
  29.0 0.0 copy-start.7
  29.0 1.5 %shard_map.113.kept = f32[10,256,256]{2,1,0:T(8,128)S(1)} custom-call(bf16[32,2,16,256]{3,2,1,0:T(8,128)(2,1)S(1)} %all-to-all-done.got, bf16[1024,512]{1,0:T(8,128)(2,1)S(1)} %get-tuple-element.31.table, f32[2,256,256]{2,1,0:T(8,128)S(1)} %get-tuple-element.32.twists), custom_call_target="tpu_custom_call" | custom-call | flops 1200000000 | bytes 4718592 | tf_op jit(solution)/shard_map/pallas_call | solution.py:212
  30.6 0.0 collective-permute-done.5.far
  30.6 0.6 collective-permute-start.6
  31.2 1.2 %collective-permute-done.6.far_pair = bf16[256,512]{1,0:T(8,128)(2,1)S(1)} collective-permute-done((bf16[256,512]{1,0:T(8,128)(2,1)S(1)}, bf16[256,512]{1,0:T(8,128)(2,1)S(1)}, u32[]{:S(2)}, u32[]{:S(2)}) %collective-permute-start.6) | collective-permute-done | bytes 262176 | tf_op jit(solution)/shard_map/ppermute | solution.py:237
  32.4 0.0 copy-done.3
  32.4 0.0 copy-done.5
  32.4 0.0 copy-done.7
  32.4 1.2 %shard_map.114 = (bf16[256,512]{1,0:T(8,128)(2,1)}, bf16[32,16,256]{2,1,0:T(8,128)(2,1)S(1)}) custom-call(bf16[2,512,512]{2,1,0:T(8,128)(2,1)S(1)} %copy-done.5, f32[256,512]{1,0:T(8,128)S(1)} %copy-done.7, bf16[256,512]{1,0:T(8,128)(2,1)S(1)} %collective-permute-done.5.far, bf16[256,512]{1,0:T(8,128)(2,1)S(1)} %collective-permute-done.6.far_pair, ...), custom_call_target="tpu_custom_call" | custom-call | flops 299999985664 | bytes 2883584 | tf_op jit(solution)/shard_map/pallas_call | solution.py:212
  33.6 0.0 copy-start
  33.6 0.0 copy-start.1
  33.6 0.0 copy-start.2
  33.6 17.6 %all_to_all.15.got = bf16[32,16,256]{2,1,0:T(8,128)(2,1)S(1)} all-to-all(bf16[32,16,256]{2,1,0:T(8,128)(2,1)S(1)} %get-tuple-element.35), channel_id=1, replica_groups=mesh['ctx'=32,'tp'=8] {'ctx'}, dimensions={0} | all-to-all | bytes 524288 | tf_op jit(solution)/shard_map/all_to_all | solution.py:240
  51.2 1.6 %shard_map.115 = bf16[32,3,16,256]{3,2,1,0:T(8,128)(2,1)S(1)} custom-call(bf16[32,16,256]{2,1,0:T(8,128)(2,1)S(1)} %all_to_all.15.got, f32[10,256,256]{2,1,0:T(8,128)S(1)} %shard_map.113.kept, bf16[1024,512]{1,0:T(8,128)(2,1)S(1)} %get-tuple-element.31.table, f32[2,256,256]{2,1,0:T(8,128)S(1)} %get-tuple-element.32.twists), custom_call_target="tpu_custom_call" | custom-call | flops 1200000000 | bytes 5242880 | tf_op jit(solution)/shard_map/pallas_call | solution.py:212
  52.8 17.4 %all_to_all.16.got = bf16[32,3,16,256]{3,2,1,0:T(8,128)(2,1)S(1)} all-to-all(bf16[32,3,16,256]{3,2,1,0:T(8,128)(2,1)S(1)} %shard_map.115), channel_id=1, replica_groups=mesh['ctx'=32,'tp'=8] {'ctx'}, dimensions={0} | all-to-all | bytes 1572864 | tf_op jit(solution)/shard_map/all_to_all | solution.py:240
  70.2 0.0 copy-done
  70.2 0.0 copy-done.1
  70.2 0.0 copy-done.2
  70.2 1.2 %shard_map.116 = (bf16[256,512]{1,0:T(8,128)(2,1)}, bf16[256,512]{1,0:T(8,128)(2,1)}, bf16[256,512]{1,0:T(8,128)(2,1)}, f32[256,512]{1,0:T(8,128)}) custom-call(bf16[32,3,16,256]{3,2,1,0:T(8,128)(2,1)S(1)} %all_to_all.16.got, bf16[256,512]{1,0:T(8,128)(2,1)S(1)} %copy-done.2, bf16[256,512]{1,0:T(8,128)(2,1)S(1)} %copy-done, bf16[256,512]{1,0:T(8,128)(2,1)S(1)} %copy-done.1), custom_call_target="tpu_custom_call" | custom-call | bytes 2883584 | tf_op jit(solution)/shard_map/pallas_call | solution.py:212
Async XLA Ops:
  0.6 3.5 %collective-permute-start.1 = (bf16[256,512]{1,0:T(8,128)(2,1)}, bf16[256,512]{1,0:T(8,128)(2,1)S(1)}, u32[]{:S(2)}, u32[]{:S(2)}) collective-permute-start(bf16[256,512]{1,0:T(8,128)(2,1)} %own.1), channel_id=1, source_target_pairs={{0,1},{1,0},{2,3},{3,2},{4,5},{5,4},{6,7},{7,6},{8,9},{9,8},{10,11... | collective-permute-start | bytes 786440 | tf_op jit(solution)/shard_map/ppermute | solution.py:237
  0.7 18.0 %collective-permute-start = (bf16[256,512]{1,0:T(8,128)(2,1)}, bf16[256,512]{1,0:T(8,128)(2,1)S(1)}, u32[]{:S(2)}, u32[]{:S(2)}) collective-permute-start(bf16[256,512]{1,0:T(8,128)(2,1)} %own.1), channel_id=1, source_target_pairs={{0,2},{1,7},{2,4},{3,1},{4,6},{5,3},{6,0},{7,5},{8,10},{9,15},{10,... | collective-permute-start | bytes 786440 | tf_op jit(solution)/shard_map/ppermute | solution.py:234
  4.1 14.6 %collective-permute-start.2 = (bf16[256,512]{1,0:T(8,128)(2,1)}, bf16[256,512]{1,0:T(8,128)(2,1)S(1)}, u32[]{:S(2)}, u32[]{:S(2)}) collective-permute-start(bf16[256,512]{1,0:T(8,128)(2,1)} %own.1), channel_id=1, source_target_pairs={{0,6},{1,3},{2,0},{3,5},{4,2},{5,7},{6,4},{7,1},{8,14},{9,11},{10,... | collective-permute-start | bytes 786440 | tf_op jit(solution)/shard_map/ppermute | solution.py:234
  10.1 18.9 %all-to-all-start = ((bf16[32,2,16,256]{3,2,1,0:T(8,128)(2,1)}), bf16[32,2,16,256]{3,2,1,0:T(8,128)(2,1)S(1)}, u32[]{:S(2)}, u32[]{:S(2)}) async-start(bf16[32,2,16,256]{3,2,1,0:T(8,128)(2,1)} %get-tuple-element.30), calls=%async_computation | async-start | bytes 1048576 | tf_op jit(solution)/shard_map/all_to_all | solution.py:240
  18.7 1.6 %collective-permute-start.3 = (bf16[256,512]{1,0:T(8,128)(2,1)S(1)}, bf16[256,512]{1,0:T(8,128)(2,1)S(1)}, u32[]{:S(2)}, u32[]{:S(2)}) collective-permute-start(bf16[256,512]{1,0:T(8,128)(2,1)S(1)} %collective-permute-done.ahead), channel_id=1, source_target_pairs={{0,1},{1,0},{2,3},{3,2},{4,5},{5,4},{6,7},{7,6},{8,9},{9,8},{10,11... | collective-permute-start | bytes 786440 | tf_op jit(solution)/shard_map/ppermute | solution.py:237
  19.1 1.6 %collective-permute-start.4 = (bf16[256,512]{1,0:T(8,128)(2,1)S(1)}, bf16[256,512]{1,0:T(8,128)(2,1)S(1)}, u32[]{:S(2)}, u32[]{:S(2)}) collective-permute-start(bf16[256,512]{1,0:T(8,128)(2,1)S(1)} %collective-permute-done.2.behind), channel_id=1, source_target_pairs={{0,1},{1,0},{2,3},{3,2},{4,5},{5,4},{6,7},{7,6},{8,9},{9,8},{10,11... | collective-permute-start | bytes 786440 | tf_op jit(solution)/shard_map/ppermute | solution.py:237
  19.3 11.2 %collective-permute-start.5 = (bf16[256,512]{1,0:T(8,128)(2,1)S(1)}, bf16[256,512]{1,0:T(8,128)(2,1)S(1)}, u32[]{:S(2)}, u32[]{:S(2)}) collective-permute-start(bf16[256,512]{1,0:T(8,128)(2,1)S(1)} %collective-permute-done.ahead), channel_id=1, source_target_pairs={{0,2},{1,7},{2,4},{3,1},{4,6},{5,3},{6,0},{7,5},{8,10},{9,15},{10,... | collective-permute-start | bytes 786440 | tf_op jit(solution)/shard_map/ppermute | solution.py:234
  22.9 1.0 %copy-start.4 = (bf16[2,512,512]{2,1,0:T(8,128)(2,1)}, bf16[2,512,512]{2,1,0:T(8,128)(2,1)S(1)}, u32[]{:S(2)}) copy-start(bf16[2,512,512]{2,1,0:T(8,128)(2,1)S(1)} %get-tuple-element.28.weight) | copy-start | bytes 3145732
  23.9 0.8 %copy-start.6 = (f32[256,512]{1,0:T(8,128)}, f32[256,512]{1,0:T(8,128)S(1)}, u32[]{:S(2)}) copy-start(f32[256,512]{1,0:T(8,128)S(1)} %get-tuple-element.33.total) | copy-start | bytes 1572868
  24.7 7.7 %copy-start.3 = (bf16[256,512]{1,0:T(8,128)(2,1)S(1)}, bf16[256,512]{1,0:T(8,128)(2,1)}, u32[]{:S(2)}) copy-start(bf16[256,512]{1,0:T(8,128)(2,1)} %gate.1) | copy-start | bytes 786436
  29.0 3.3 %copy-start.5 = (bf16[2,512,512]{2,1,0:T(8,128)(2,1)S(1)}, bf16[2,512,512]{2,1,0:T(8,128)(2,1)}, u32[]{:S(2)}) copy-start(bf16[2,512,512]{2,1,0:T(8,128)(2,1)} %copy-done.4) | copy-start | bytes 3145732
  29.0 3.3 %copy-start.7 = (f32[256,512]{1,0:T(8,128)S(1)}, f32[256,512]{1,0:T(8,128)}, u32[]{:S(2)}) copy-start(f32[256,512]{1,0:T(8,128)} %copy-done.6) | copy-start | bytes 1572868
  30.6 1.8 %collective-permute-start.6 = (bf16[256,512]{1,0:T(8,128)(2,1)S(1)}, bf16[256,512]{1,0:T(8,128)(2,1)S(1)}, u32[]{:S(2)}, u32[]{:S(2)}) collective-permute-start(bf16[256,512]{1,0:T(8,128)(2,1)S(1)} %collective-permute-done.5.far), channel_id=1, source_target_pairs={{0,1},{1,0},{2,3},{3,2},{4,5},{5,4},{6,7},{7,6},{8,9},{9,8},{10,11... | collective-permute-start | bytes 786440 | tf_op jit(solution)/shard_map/ppermute | solution.py:237
  33.6 36.6 %copy-start = (bf16[256,512]{1,0:T(8,128)(2,1)S(1)}, bf16[256,512]{1,0:T(8,128)(2,1)}, u32[]{:S(2)}) copy-start(bf16[256,512]{1,0:T(8,128)(2,1)} %key.3) | copy-start | bytes 786436
  33.6 36.6 %copy-start.1 = (bf16[256,512]{1,0:T(8,128)(2,1)S(1)}, bf16[256,512]{1,0:T(8,128)(2,1)}, u32[]{:S(2)}) copy-start(bf16[256,512]{1,0:T(8,128)(2,1)} %value.3) | copy-start | bytes 786436
  33.6 36.6 %copy-start.2 = (bf16[256,512]{1,0:T(8,128)(2,1)S(1)}, bf16[256,512]{1,0:T(8,128)(2,1)}, u32[]{:S(2)}) copy-start(bf16[256,512]{1,0:T(8,128)(2,1)} %get-tuple-element.37.mix) | copy-start | bytes 786436

commit v4 on v3

--- a/solution.py
+++ b/solution.py
@@ -13,6 +13,7 @@
 F32 = jnp.float32
 PARTS = 32
 ROWS = 256
+SIDE = PARTS // 2
 CHANS = 16
 TOKENS = PARTS * ROWS
 HALF = CHANS // 2
@@ -32,8 +33,7 @@
     cos, sin = np.cos(second), np.sin(second)
     ahead = np.block([[cos, -sin], [sin, cos]])
     packed = np.concatenate([ahead, gather, np.concatenate([spread_re, spread_im], 1)], 0)
-    wide = lambda a: np.broadcast_to(a[:, None, :], (PARTS, HALF, ROWS)).reshape(WIDE, ROWS)
-    twists = np.stack([wide(np.cos(twist)), wide(np.sin(twist))])
+    twists = np.stack([np.cos(twist), np.sin(twist)])
     return packed.astype(ml_dtypes.bfloat16), twists.astype(np.float32)
 
 
@@ -45,21 +45,28 @@
     return lax.dot_general(a, b, (((1,), (1,)), ((), ())), preferred_element_type=F32)
 
 
-def spectra(signals, table, twists):
+def widen(twists):
+    return [
+        jnp.broadcast_to(twists[n][:, None, :], (PARTS, HALF, ROWS)).reshape(WIDE, ROWS)
+        for n in range(2)
+    ]
+
+
+def first_stage(signals, spread, twists):
     cos, sin = twists[0], twists[1]
     turned = []
     for signal in signals:
-        re = dot(table[2 * ROWS + WIDE :, :WIDE], signal)
-        im = dot(table[2 * ROWS + WIDE :, WIDE:], signal)
+        re = dot(spread[:, :WIDE], signal)
+        im = dot(spread[:, WIDE:], signal)
         turned.append(
             jnp.concatenate([(re * cos + im * sin).astype(BF), (im * cos - re * sin).astype(BF)], 1)
         )
-    return dot(jnp.concatenate(turned, 0), table[: 2 * ROWS, :])
-
-
-def inverses(pairs, table, twists):
+    return jnp.concatenate(turned, 0)
+
+
+def inverses(pairs, ahead, gather, twists):
     rows = [jnp.concatenate([re.astype(BF), minus_im.astype(BF)], 1) for re, minus_im in pairs]
-    out = dot(jnp.concatenate(rows, 0), table[: 2 * ROWS, :])
+    out = dot(jnp.concatenate(rows, 0), ahead[...])
     cos, sin = twists[0], twists[1]
     results = []
     for n in range(len(pairs)):
@@ -67,9 +74,24 @@
         minus_im = out[n * WIDE : (n + 1) * WIDE, ROWS:]
         turned_re = (re * cos + minus_im * sin).astype(BF)
         turned_im = (re * sin - minus_im * cos).astype(BF)
-        back = dot(table[2 * ROWS : 2 * ROWS + WIDE, :], jnp.concatenate([turned_re, turned_im], 0))
+        back = dot(gather[...], jnp.concatenate([turned_re, turned_im], 0))
         results.append((back * SCALE).reshape(PARTS, HALF, ROWS))
     return results
+
+
+def load_tables(table, twists, held, held_twists, sems):
+    first = 2 * ROWS + WIDE
+    ends = [
+        (table.at[first:], held.at[first:]),
+        (twists, held_twists),
+        (table.at[: 2 * ROWS], held.at[: 2 * ROWS]),
+        (table.at[2 * ROWS : first], held.at[2 * ROWS : first]),
+    ]
+    loads = [pltpu.make_async_copy(*pair, sems.at[n]) for n, pair in enumerate(ends)]
+    for load in loads:
+        load.start()
+    parts = (held.at[first:], held.at[: 2 * ROWS], held.at[2 * ROWS : first])
+    return loads, parts
 
 
 def halves(block):
@@ -81,33 +103,96 @@
     return jnp.stack(parts, 1).reshape(PARTS, CHANS, ROWS).astype(BF)
 
 
-KEPT = 5
-
-
-def early_kernel(got, table, twists, kept):
-    out = spectra(halves(got[:, 0]) + halves(got[:, 1]), table, twists)
+KEPT = 4
+TABLE = 4
+CONV, TABLES = 8, 10
+
+
+def pick_kernel(got, stay, away, sems):
+    copies = [pltpu.make_async_copy(got.at[:, n], out, sems.at[n]) for n, out in enumerate((stay, away))]
+    for copy in copies:
+        copy.start()
+    for copy in copies:
+        copy.wait()
+
+
+def start_all(ends, sems):
+    copies = [pltpu.make_async_copy(*pair, sems.at[n]) for n, pair in enumerate(ends)]
+    for copy in copies:
+        copy.start()
+    return copies
+
+
+def wait_all(copies):
+    for copy in copies:
+        copy.wait()
+
+
+SPREAD = slice(2 * ROWS + WIDE, 2 * ROWS + 2 * WIDE)
+AHEAD = slice(0, 2 * ROWS)
+GATHER = slice(2 * ROWS, 2 * ROWS + WIDE)
+
+
+class Parts:
+    def __init__(self, refs):
+        self.where = [(ref, n) for ref in refs for n in range(ref.shape[0])]
+
+    def put(self, index, value):
+        ref, n = self.where[index]
+        ref[n] = value.astype(ref.dtype)
+
+    def get(self, index, dtype=F32):
+        ref, n = self.where[index]
+        return ref[n].astype(dtype)
+
+
+def early_kernel(near, other, table, twists, *refs):
+    kept, (kept_twists, both, tab, tw, sems) = Parts(refs[:-5]), refs[-5:]
+    side = lax.div(lax.axis_index("ctx"), SIDE)
+    ends = [(near, both.at[side]), (other, both.at[1 - side]), (table, tab), (twists, tw)]
+    wait_all(start_all(ends, sems))
+    got = both[...].reshape(PARTS, 2, CHANS, ROWS)
+    signals = halves(got[:, 0]) + halves(got[:, 1])
+    wide = widen(tw)
+    out = dot(first_stage(signals, tab.at[SPREAD], wide), tab[AHEAD, :])
     pairs = []
     for half in range(2):
         x, h = out[half * WIDE : (half + 1) * WIDE], out[(half + 2) * WIDE : (half + 3) * WIDE]
         xr, xi, hr, hi = x[:, :ROWS], x[:, ROWS:], h[:, :ROWS], h[:, ROWS:]
         for n, part in enumerate((xr, xi, hr, hi)):
-            kept[half * KEPT + n] = part
+            kept.put(half * KEPT + n, part)
         pairs.append((hr * xr - hi * xi, -(hr * xi + hi * xr)))
-    for half, conv in enumerate(inverses(pairs, table, twists)):
-        kept[half * KEPT + 4] = conv.reshape(WIDE, ROWS)
-
-
-def late_kernel(got, kept, table, twists, out):
-    out[:, 0] = whole([kept[half * KEPT + 4].reshape(PARTS, HALF, ROWS) for half in range(2)])
-    grad = spectra(halves(got[...]), table, twists)
+    for half, conv in enumerate(inverses(pairs, tab.at[AHEAD], tab.at[GATHER], wide)):
+        kept.put(CONV + half, conv.reshape(WIDE, ROWS))
+    for side in range(2):
+        for n in range(TABLE):
+            rows, cols = slice(n * ROWS, (n + 1) * ROWS), slice(side * ROWS, (side + 1) * ROWS)
+            kept.put(TABLES + side * TABLE + n, tab[rows, cols])
+    kept_twists[...] = tw[...]
+
+
+def late_kernel(got, *refs):
+    kept, (twists, out) = Parts(refs[:-2]), refs[-2:]
+
+    def table(start, stop):
+        sides = [
+            jnp.concatenate([kept.get(TABLES + side * TABLE + n, BF) for n in range(start, stop)], 0)
+            for side in range(2)
+        ]
+        return jnp.concatenate(sides, 1)
+
+    ahead, gather, spread = table(0, 2), table(2, 3), table(3, 4)
+    twists = widen(twists)
+    out[:, 0] = whole([kept.get(CONV + n).reshape(PARTS, HALF, ROWS) for n in range(2)])
+    grad = dot(first_stage(halves(got[...]), spread, twists), ahead)
     pairs = []
     for half in range(2):
         g = grad[half * WIDE : (half + 1) * WIDE]
         gr, gi = g[:, :ROWS], g[:, ROWS:]
-        xr, xi, hr, hi = (kept[half * KEPT + n] for n in range(4))
+        xr, xi, hr, hi = (kept.get(half * KEPT + n) for n in range(KEPT))
         pairs.append((hr * gr + hi * gi, hi * gr - hr * gi))
         pairs.append((xr * gr + xi * gi, xi * gr - xr * gi))
-    results = inverses(pairs, table, twists)
+    results = inverses(pairs, ahead, gather, twists)
     out[:, 1] = whole([results[0], results[2]])
     out[:, 2] = whole([results[1], results[3]])
 
@@ -121,29 +206,32 @@
 
 
 def prepare_kernel(
-    key, value, taps, own, weight, table, twists, pair,
-    out, total, table_out, twists_out, k, v, t, o, w, sent, sems,
+    key, value, taps, own, weight, pair, out, total, k, v, t, o, w, sent, sems
 ):
     width = own.shape[1]
     loads = [(key, k), (value, v), (taps, t), (own, o)]
     loads += [(weight.at[:, columns(0, flip, width)], w.at[flip]) for flip in range(2)]
-    loads += [(table, table_out), (twists, twists_out)]
     loads = [pltpu.make_async_copy(*ends, sems.at[n]) for n, ends in enumerate(loads)]
     for load in loads:
         load.start()
     for load in loads[:2]:
         load.wait()
     inner = k[...].astype(F32) * v[...].astype(F32)
-    sent[:, 0] = inner.T.astype(BF).reshape(PARTS, CHANS, ROWS)
+    side = lax.div(lax.axis_index("ctx"), SIDE)
+
+    def place(signal, block):
+        parts = block.T.astype(BF).reshape(2, SIDE, CHANS, ROWS)
+        for owner in range(2):
+            sent[:, owner ^ side, signal] = parts[owner]
+
+    place(0, inner)
     loads[2].wait()
-    sent[:, 1] = t[...].T.astype(BF).reshape(PARTS, CHANS, ROWS)
-    store = pltpu.make_async_copy(sent, out, sems.at[8])
+    place(1, t[...])
+    store = pltpu.make_async_copy(sent, out, sems.at[6])
     store.start()
-    for load in loads[3:6]:
+    for load in loads[3:]:
         load.wait()
     total[...] = dot_t(o[...], w[0]) + dot_t(pair[...], w[1])
-    for load in loads[6:]:
-        load.wait()
     store.wait()
 
 
@@ -165,14 +253,24 @@
     loads[5].wait()
 
 
-def last_mix_kernel(weight, total, far, far_pair, gate, mix, out, mixed, sem):
-    sums = total[...] + dot_t(far[...], weight[0]) + dot_t(far_pair[...], weight[1])
-    mixed[...] = sums.astype(BF)
-    store = pltpu.make_async_copy(mixed, mix, sem)
-    store.start()
-    grad = sums.astype(BF).astype(F32) * gate[...].astype(F32)
-    out[...] = grad.T.astype(BF).reshape(PARTS, CHANS, ROWS)
-    store.wait()
+def last_mix_kernel(weight, total, far, far_pair, gate, mix, out, mixed, grads, sems):
+    width = total.shape[1] // 2
+    copies = []
+    for n in range(2):
+        chans = slice(n * width, (n + 1) * width)
+        sums = total[:, chans] + dot_t(far[...], weight[0, chans, :])
+        sums = sums + dot_t(far_pair[...], weight[1, chans, :])
+        mixed[n] = sums.astype(BF)
+        grad = mixed[n].astype(F32) * gate[:, chans].astype(F32)
+        grads[n] = grad.T.astype(BF).reshape(PARTS // 2, CHANS, ROWS)
+        copies.append(
+            pltpu.make_async_copy(grads.at[n], out.at[n * PARTS // 2 : (n + 1) * PARTS // 2], sems.at[n])
+        )
+        copies[-1].start()
+        copies.append(pltpu.make_async_copy(mixed.at[n], mix.at[:, chans], sems.at[2 + n]))
+        copies[-1].start()
+    for copy in copies:
+        copy.wait()
 
 
 def finish_kernel(got, mix, key, value, *refs):
@@ -245,24 +343,29 @@
     partial = shape((rows, chans), F32)
     held = pltpu.VMEM((rows, chans), BF)
     weights = lambda n: (n, chans, chans)
-    sems = pltpu.SemaphoreType.DMA((14,))
+    sems = pltpu.SemaphoreType.DMA((7,))
+
+    tables_held = [pltpu.VMEM(table.shape, BF), pltpu.VMEM(twists.shape, F32)]
 
     ahead = ring(out_grad, 1)
     pair = swap(out_grad)
     again, pair = together((out_grad, pair))
     behind = ring(again, -1)
-    sent, total, table, twists = call(
+    sent, total = call(
         prepare_kernel,
-        (shape((PARTS, 2, CHANS, ROWS)), partial, shape(table.shape), shape(twists.shape, F32)),
-        key_act, value_act, filter_taps, out_grad, out_weight, table, twists, pair,
-        spaces="hhhhhhhv" + "hvvv",
+        (shape((SIDE, 2, 2, CHANS, ROWS)), partial),
+        key_act, value_act, filter_taps, out_grad, out_weight, pair,
+        spaces="hhhhhv" + "hv",
         scratch=[
             held, held, pltpu.VMEM((rows, chans), F32), held, pltpu.VMEM(weights(2), BF),
-            pltpu.VMEM((PARTS, 2, CHANS, ROWS), BF), sems,
+            pltpu.VMEM((SIDE, 2, 2, CHANS, ROWS), BF), sems,
         ],
         flops=270_000_000,
     )
-    got = exchange(sent)
+    planes = [list(range(SIDE)), list(range(SIDE, PARTS))]
+    near = lax.all_to_all(
+        sent, "ctx", split_axis=0, concat_axis=0, tiled=True, axis_index_groups=planes
+    )
     ahead, total = together((ahead, total))
     far = ring(ahead, 1)
     ahead, behind = together((ahead, behind))
@@ -272,22 +375,31 @@
         spaces="hvvvvv" + "vv",
         scratch=[pltpu.VMEM(weights(4), BF), sems], flops=7_000_000_000,
     )
-    kept = call(
-        early_kernel, shape((2 * KEPT, WIDE, ROWS), F32), got, table, twists,
-        spaces="vvv" + "v",
-        flops=1_200_000_000,
-    )
-    far, total, kept = together((far, total, kept))
+    near, away = call(
+        pick_kernel, (shape((SIDE, 2, CHANS, ROWS)), shape((SIDE, 2, CHANS, ROWS))), near,
+        spaces="v" + "hh", scratch=[sems],
+    )
+    far, total, away = together((far, total, away))
+    other = lax.ppermute(away, "ctx", [(i, (i + SIDE) % PARTS) for i in range(PARTS)])
     mix, sent = call(
         last_mix_kernel, (shape((rows, chans)), block),
         later, total, far, swap(far), gate_act,
-        spaces="vvvvv" + "hv",
-        scratch=[held, pltpu.SemaphoreType.DMA], flops=300_000_000_000,
+        spaces="vvvvv" + "hh",
+        scratch=[
+            pltpu.VMEM((2, rows, chans // 2), BF), pltpu.VMEM((2, PARTS // 2, CHANS, ROWS), BF), sems,
+        ],
+        flops=300_000_000_000,
     )
     got = exchange(sent)
+    kept = call(
+        early_kernel, (shape((10, WIDE, ROWS)), shape((8, WIDE, ROWS)), shape(twists.shape, F32)), near, other, table, twists,
+        spaces="hhhh" + "vvv",
+        scratch=[pltpu.VMEM((2, SIDE, 2, CHANS, ROWS), BF), *tables_held, sems],
+        flops=20_000_000_000,
+    )
     sent = call(
-        late_kernel, shape((PARTS, 3, CHANS, ROWS)), got, kept, table, twists,
-        spaces="vvvv" + "v", flops=1_200_000_000,
+        late_kernel, shape((PARTS, 3, CHANS, ROWS)), got, *kept,
+        spaces="v" + "vvv" + "v", flops=1_200_000_000,
     )
     got = exchange(sent)
     return tuple(call(

time: 71.7 us -> 70.5 us (0.983)
  blocking collectives: 34.9 us -> 17.4 us
  starting transfers between devices: 17.7 us -> 25.5 us
  waiting for transfers between devices: 6.22 us -> 14 us
  Pallas kernels: 9.99 us -> 12.5 us
  local copies, waits for them, and re-layouts: 1.82 us -> 0.03 us
    all_to_all x2 -> x1, blocking collectives: 34.9 us -> 17.4 us  [exchange(): return lax.all_to_all(block, 'ctx', split_axis=0, concat_axis=0, tiled=True)]
    all_to_all x0 -> x1, waiting for transfers between devices: none -> 7.29 us  [shards(): lax.all_to_all(sent, 'ctx', split_axis=0, concat_axis=0, tiled=True, axis...]
    all_to_all x0 -> x1, starting transfers between devices: none -> 7.05 us  [shards(): lax.all_to_all(sent, 'ctx', split_axis=0, concat_axis=0, tiled=True, axis...]
    pallas_call x6 -> x7, Pallas kernels: 9.99 us -> 12.5 us  [call(): pl.pallas_call(kernel, out_shape=placed, in_specs=specs[:len(args)], out_...]
    unnamed x16 -> x8, local copies, waits for them, and re-layouts: 1.82 us -> 0.03 us
    ppermute x4, waiting for transfers between devices: 1.9 us -> 0.43 us  [swap(): return lax.ppermute(block, 'tp', [(i, i ^ 1) for i in range(count)])]
    ppermute x0 -> x1, starting transfers between devices: none -> 1.1 us  [shards(): lax.ppermute(away, 'ctx', [(i, (i + SIDE) % PARTS) for i in range(PARTS)])]
    ppermute x3, waiting for transfers between devices: 0.01 us -> 0.97 us  [ring(): return lax.ppermute(block, 'tp', hops)]
  transfers between devices with their start and end apart: 8 -> 10, of which waited for: 4 -> 4; matrix products, arithmetic and copies ran while one was open for 0% -> 0% of each run, Pallas kernels for 8% -> 14%
where the time goes in v4:
time: 70.5 us; the launch traced here: 70.1 us
  starting transfers between devices  25.5 us (36%)
  blocking collectives  17.4 us (25%)
  waiting for transfers between devices  14 us (20%)
  Pallas kernels  12.5 us (18%)
  between operations  0.78 us (1%)
    all_to_all x1, blocking collectives, exchange(): return lax.all_to_all(block, 'ctx', split_axis=0, concat_axis=0, tiled=True)  17.4 us
    pallas_call x7, Pallas kernels, call(): pl.pallas_call(kernel, out_shape=placed, in_specs=specs[:len(args)], out_...  12.5 us
    all_to_all x1, starting transfers between devices, exchange(): return lax.all_to_all(block, 'ctx', split_axis=0, concat_axis=0, tiled=True)  8.14 us
    ppermute x3, starting transfers between devices, ring(): return lax.ppermute(block, 'tp', hops)  8.09 us
    all_to_all x1, waiting for transfers between devices, shards(): lax.all_to_all(sent, 'ctx', split_axis=0, concat_axis=0, tiled=True, axis...  7.29 us
    all_to_all x1, starting transfers between devices, shards(): lax.all_to_all(sent, 'ctx', split_axis=0, concat_axis=0, tiled=True, axis...  7.05 us
    all_to_all x1, waiting for transfers between devices, exchange(): return lax.all_to_all(block, 'ctx', split_axis=0, concat_axis=0, tiled=True)  5.26 us
  transfers between devices with their start and end apart: 10, of which 4 were waited for; matrix products, arithmetic and copies ran while one was open for 0% of the time, Pallas kernels for 14%

profile of v4, /device:TPU:32, one launch (start us, length us, event | category | flops | bytes accessed | tf_op | source)
XLA Modules:
  0.0 70.1 jit_solution(10603882306080219944)
XLA Ops:
  0.6 0.1 collective-permute-start.1
  0.7 3.3 %collective-permute-start = (bf16[256,512]{1,0:T(8,128)(2,1)}, bf16[256,512]{1,0:T(8,128)(2,1)S(1)}, u32[]{:S(2)}, u32[]{:S(2)}) collective-permute-start(bf16[256,512]{1,0:T(8,128)(2,1)} %own.1), channel_id=1, source_target_pairs={{0,2},{1,7},{2,4},{3,1},{4,6},{5,3},{6,0},{7,5},{8,10},{9,15},{10,... | collective-permute-start | bytes 786440 | tf_op jit(solution)/shard_map/ppermute | solution.py:332
  4.1 0.0 collective-permute-done.1.pair
  4.1 3.8 %collective-permute-start.2 = (bf16[256,512]{1,0:T(8,128)(2,1)}, bf16[256,512]{1,0:T(8,128)(2,1)S(1)}, u32[]{:S(2)}, u32[]{:S(2)}) collective-permute-start(bf16[256,512]{1,0:T(8,128)(2,1)} %own.1), channel_id=1, source_target_pairs={{0,6},{1,3},{2,0},{3,5},{4,2},{5,7},{6,4},{7,1},{8,14},{9,11},{10,... | collective-permute-start | bytes 786440 | tf_op jit(solution)/shard_map/ppermute | solution.py:332
  7.9 2.2 %shard_map.111 = (bf16[16,2,2,16,256]{4,3,2,1,0:T(8,128)(2,1)}, f32[256,512]{1,0:T(8,128)S(1)}) custom-call(bf16[256,512]{1,0:T(8,128)(2,1)} %key.3, bf16[256,512]{1,0:T(8,128)(2,1)} %value.3, f32[256,512]{1,0:T(8,128)} %taps.1, bf16[256,512]{1,0:T(8,128)(2,1)} %own.1, bf16[512,4096]{1,0:T(8,128)(2,1)} %weight.3, ...), custom_call_target="tpu_custom_call" | custom-call | flops 270000000 | bytes 6815744 | tf_op jit(solution)/shard_map/pallas_call | solution.py:310
  10.1 7.0 %all-to-all-start = ((bf16[16,2,2,16,256]{4,3,2,1,0:T(8,128)(2,1)}), bf16[16,2,2,16,256]{4,3,2,1,0:T(8,128)(2,1)S(1)}, u32[]{:S(2)}, u32[]{:S(2)}) async-start(bf16[16,2,2,16,256]{4,3,2,1,0:T(8,128)(2,1)} %get-tuple-element.33), calls=%async_computation | async-start | bytes 1048576 | tf_op jit(solution)/shard_map/all_to_all | solution.py:366
  17.1 1.0 %collective-permute-done.ahead = bf16[256,512]{1,0:T(8,128)(2,1)S(1)} collective-permute-done((bf16[256,512]{1,0:T(8,128)(2,1)}, bf16[256,512]{1,0:T(8,128)(2,1)S(1)}, u32[]{:S(2)}, u32[]{:S(2)}) %collective-permute-start) | collective-permute-done | bytes 262176 | tf_op jit(solution)/shard_map/ppermute | solution.py:332
  18.1 0.0 collective-permute-done.2.behind
  18.1 0.9 %collective-permute-start.3 = (bf16[256,512]{1,0:T(8,128)(2,1)S(1)}, bf16[256,512]{1,0:T(8,128)(2,1)S(1)}, u32[]{:S(2)}, u32[]{:S(2)}) collective-permute-start(bf16[256,512]{1,0:T(8,128)(2,1)S(1)} %collective-permute-done.ahead), channel_id=1, source_target_pairs={{0,1},{1,0},{2,3},{3,2},{4,5},{5,4},{6,7},{7,6},{8,9},{9,8},{10,11... | collective-permute-start | bytes 786440 | tf_op jit(solution)/shard_map/ppermute | solution.py:335
  19.0 0.0 collective-permute-start.4
  19.0 1.0 %collective-permute-start.5 = (bf16[256,512]{1,0:T(8,128)(2,1)S(1)}, bf16[256,512]{1,0:T(8,128)(2,1)S(1)}, u32[]{:S(2)}, u32[]{:S(2)}) collective-permute-start(bf16[256,512]{1,0:T(8,128)(2,1)S(1)} %collective-permute-done.ahead), channel_id=1, source_target_pairs={{0,2},{1,7},{2,4},{3,1},{4,6},{5,3},{6,0},{7,5},{8,10},{9,15},{10,... | collective-permute-start | bytes 786440 | tf_op jit(solution)/shard_map/ppermute | solution.py:332
  20.0 7.3 %all-to-all-done.got = bf16[16,2,2,16,256]{4,3,2,1,0:T(8,128)(2,1)S(1)} async-done(((bf16[16,2,2,16,256]{4,3,2,1,0:T(8,128)(2,1)}), bf16[16,2,2,16,256]{4,3,2,1,0:T(8,128)(2,1)S(1)}, u32[]{:S(2)}, u32[]{:S(2)}) %all-to-all-start) | async-done | bytes 524320 | tf_op jit(solution)/shard_map/all_to_all | solution.py:366
  27.3 0.8 %shard_map.113 = (bf16[16,2,16,256]{3,2,1,0:T(8,128)(2,1)}, bf16[16,2,16,256]{3,2,1,0:T(8,128)(2,1)}) custom-call(bf16[16,2,2,16,256]{4,3,2,1,0:T(8,128)(2,1)S(1)} %all-to-all-done.got), custom_call_target="tpu_custom_call" | custom-call | bytes 1048576 | tf_op jit(solution)/shard_map/pallas_call | solution.py:310
  28.1 0.0 copy-start.3
  28.1 0.0 collective-permute-done.3.ahead_pair
  28.2 0.0 collective-permute-done.4.behind_pair
  28.2 2.2 %shard_map.112 = (f32[256,512]{1,0:T(8,128)S(1)}, bf16[2,512,512]{2,1,0:T(8,128)(2,1)S(1)}) custom-call(bf16[512,4096]{1,0:T(8,128)(2,1)} %weight.3, f32[256,512]{1,0:T(8,128)S(1)} %get-tuple-element.26.before, bf16[256,512]{1,0:T(8,128)(2,1)S(1)} %collective-permute-done.ahead, bf16[256,512]{1,0:T(8,128)(2,1)S(1)} %collective-permute-done.3.ahead_pair, ...), custom_call_target="tpu_custom_call" | custom-call | flops 7000000000 | bytes 7340032 | tf_op jit(solution)/shard_map/pallas_call | solution.py:310
  30.3 0.0 collective-permute-done.5.far
  30.3 0.1 collective-permute-start.6
  30.4 1.1 %collective-permute-start.7 = (bf16[16,2,16,256]{3,2,1,0:T(8,128)(2,1)}, bf16[16,2,16,256]{3,2,1,0:T(8,128)(2,1)}, u32[]{:S(2)}, u32[]{:S(2)}) collective-permute-start(bf16[16,2,16,256]{3,2,1,0:T(8,128)(2,1)} %get-tuple-element.39), channel_id=1, source_target_pairs={{0,128},{8,136},{16,144},{24,152},{32,160},{40,168},{48,176},{56,1... | collective-permute-start | bytes 786440 | tf_op jit(solution)/shard_map/ppermute | solution.py:383
  31.5 0.4 collective-permute-done.6.far_pair
  32.0 0.0 copy-done.3
  32.0 1.4 %shard_map.114 = (bf16[256,512]{1,0:T(8,128)(2,1)}, bf16[32,16,256]{2,1,0:T(8,128)(2,1)}) custom-call(bf16[2,512,512]{2,1,0:T(8,128)(2,1)S(1)} %get-tuple-element.31.weight, f32[256,512]{1,0:T(8,128)S(1)} %get-tuple-element.35.total, bf16[256,512]{1,0:T(8,128)(2,1)S(1)} %collective-permute-done.5.far, bf16[256,512]{1,0:T(8,128)(2,1)S(1)} %collective-permute-done.6.far_pair, ...), custom_call_target="tpu_custom_call" | custom-call | flops 299999985664 | bytes 2883584 | tf_op jit(solution)/shard_map/pallas_call | solution.py:310
  33.4 8.1 %all-to-all-start.1 = ((bf16[32,16,256]{2,1,0:T(8,128)(2,1)}), bf16[32,16,256]{2,1,0:T(8,128)(2,1)S(1)}, u32[]{:S(2)}, u32[]{:S(2)}) async-start(bf16[32,16,256]{2,1,0:T(8,128)(2,1)} %get-tuple-element.37), calls=%async_computation.1 | async-start | bytes 524288 | tf_op jit(solution)/shard_map/all_to_all | solution.py:338
  41.5 0.0 collective-permute-done.7.other
  41.5 3.1 %shard_map.115 = (bf16[10,256,256]{2,1,0:T(8,128)(2,1)S(1)}, bf16[8,256,256]{2,1,0:T(8,128)(2,1)S(1)}, f32[2,32,256]{2,1,0:T(8,128)S(1)}) custom-call(bf16[16,2,16,256]{3,2,1,0:T(8,128)(2,1)} %get-tuple-element.38.near, bf16[16,2,16,256]{3,2,1,0:T(8,128)(2,1)} %collective-permute-done.7.other, bf16[1024,512]{1,0:T(8,128)(2,1)} %constant.4.clone.table, ...), custom_call_target="tpu_custom_call" | custom-call | flops 20000000000 | bytes 4063232 | tf_op jit(solution)/shard_map/pallas_call | solution.py:310
  44.6 0.0 copy-start
  44.6 0.0 copy-start.1
  44.6 0.0 copy-start.2
  44.6 5.3 %all-to-all-done.1.got = bf16[32,16,256]{2,1,0:T(8,128)(2,1)S(1)} async-done(((bf16[32,16,256]{2,1,0:T(8,128)(2,1)}), bf16[32,16,256]{2,1,0:T(8,128)(2,1)S(1)}, u32[]{:S(2)}, u32[]{:S(2)}) %all-to-all-start.1) | async-done | bytes 262176 | tf_op jit(solution)/shard_map/all_to_all | solution.py:338
  49.9 1.6 %shard_map.116 = bf16[32,3,16,256]{3,2,1,0:T(8,128)(2,1)S(1)} custom-call(bf16[32,16,256]{2,1,0:T(8,128)(2,1)S(1)} %all-to-all-done.1.got, bf16[10,256,256]{2,1,0:T(8,128)(2,1)S(1)} %get-tuple-element.40.refs_0_, bf16[8,256,256]{2,1,0:T(8,128)(2,1)S(1)} %get-tuple-element.41.refs_1_, f32[2,32,256]{2,1,0:T(8,128)S(1)} %get-tuple-element.42.refs_2_), custom_call_target="tpu_custom_call" | custom-call | flops 1200000000 | bytes 3473408 | tf_op jit(solution)/shard_map/pallas_call | solution.py:310
  51.5 17.4 %all_to_all.15.got = bf16[32,3,16,256]{3,2,1,0:T(8,128)(2,1)S(1)} all-to-all(bf16[32,3,16,256]{3,2,1,0:T(8,128)(2,1)S(1)} %shard_map.116), channel_id=1, replica_groups=mesh['ctx'=32,'tp'=8] {'ctx'}, dimensions={0} | all-to-all | bytes 1572864 | tf_op jit(solution)/shard_map/all_to_all | solution.py:338
  68.9 0.0 copy-done
  68.9 0.0 copy-done.1
  68.9 0.0 copy-done.2
  68.9 1.2 %shard_map.117 = (bf16[256,512]{1,0:T(8,128)(2,1)}, bf16[256,512]{1,0:T(8,128)(2,1)}, bf16[256,512]{1,0:T(8,128)(2,1)}, f32[256,512]{1,0:T(8,128)}) custom-call(bf16[32,3,16,256]{3,2,1,0:T(8,128)(2,1)S(1)} %all_to_all.15.got, bf16[256,512]{1,0:T(8,128)(2,1)S(1)} %copy-done.2, bf16[256,512]{1,0:T(8,128)(2,1)S(1)} %copy-done, bf16[256,512]{1,0:T(8,128)(2,1)S(1)} %copy-done.1), custom_call_target="tpu_custom_call" | custom-call | bytes 2883584 | tf_op jit(solution)/shard_map/pallas_call | solution.py:310
Async XLA Ops:
  0.6 3.5 %collective-permute-start.1 = (bf16[256,512]{1,0:T(8,128)(2,1)}, bf16[256,512]{1,0:T(8,128)(2,1)S(1)}, u32[]{:S(2)}, u32[]{:S(2)}) collective-permute-start(bf16[256,512]{1,0:T(8,128)(2,1)} %own.1), channel_id=1, source_target_pairs={{0,1},{1,0},{2,3},{3,2},{4,5},{5,4},{6,7},{7,6},{8,9},{9,8},{10,11... | collective-permute-start | bytes 786440 | tf_op jit(solution)/shard_map/ppermute | solution.py:335
  0.7 17.4 %collective-permute-start = (bf16[256,512]{1,0:T(8,128)(2,1)}, bf16[256,512]{1,0:T(8,128)(2,1)S(1)}, u32[]{:S(2)}, u32[]{:S(2)}) collective-permute-start(bf16[256,512]{1,0:T(8,128)(2,1)} %own.1), channel_id=1, source_target_pairs={{0,2},{1,7},{2,4},{3,1},{4,6},{5,3},{6,0},{7,5},{8,10},{9,15},{10,... | collective-permute-start | bytes 786440 | tf_op jit(solution)/shard_map/ppermute | solution.py:332
  4.1 14.0 %collective-permute-start.2 = (bf16[256,512]{1,0:T(8,128)(2,1)}, bf16[256,512]{1,0:T(8,128)(2,1)S(1)}, u32[]{:S(2)}, u32[]{:S(2)}) collective-permute-start(bf16[256,512]{1,0:T(8,128)(2,1)} %own.1), channel_id=1, source_target_pairs={{0,6},{1,3},{2,0},{3,5},{4,2},{5,7},{6,4},{7,1},{8,14},{9,11},{10,... | collective-permute-start | bytes 786440 | tf_op jit(solution)/shard_map/ppermute | solution.py:332
  10.1 17.2 %all-to-all-start = ((bf16[16,2,2,16,256]{4,3,2,1,0:T(8,128)(2,1)}), bf16[16,2,2,16,256]{4,3,2,1,0:T(8,128)(2,1)S(1)}, u32[]{:S(2)}, u32[]{:S(2)}) async-start(bf16[16,2,2,16,256]{4,3,2,1,0:T(8,128)(2,1)} %get-tuple-element.33), calls=%async_computation | async-start | bytes 1048576 | tf_op jit(solution)/shard_map/all_to_all | solution.py:366
  18.1 10.1 %collective-permute-start.3 = (bf16[256,512]{1,0:T(8,128)(2,1)S(1)}, bf16[256,512]{1,0:T(8,128)(2,1)S(1)}, u32[]{:S(2)}, u32[]{:S(2)}) collective-permute-start(bf16[256,512]{1,0:T(8,128)(2,1)S(1)} %collective-permute-done.ahead), channel_id=1, source_target_pairs={{0,1},{1,0},{2,3},{3,2},{4,5},{5,4},{6,7},{7,6},{8,9},{9,8},{10,11... | collective-permute-start | bytes 786440 | tf_op jit(solution)/shard_map/ppermute | solution.py:335
  19.0 9.1 %collective-permute-start.4 = (bf16[256,512]{1,0:T(8,128)(2,1)S(1)}, bf16[256,512]{1,0:T(8,128)(2,1)S(1)}, u32[]{:S(2)}, u32[]{:S(2)}) collective-permute-start(bf16[256,512]{1,0:T(8,128)(2,1)S(1)} %collective-permute-done.2.behind), channel_id=1, source_target_pairs={{0,1},{1,0},{2,3},{3,2},{4,5},{5,4},{6,7},{7,6},{8,9},{9,8},{10,11... | collective-permute-start | bytes 786440 | tf_op jit(solution)/shard_map/ppermute | solution.py:335
  19.0 11.3 %collective-permute-start.5 = (bf16[256,512]{1,0:T(8,128)(2,1)S(1)}, bf16[256,512]{1,0:T(8,128)(2,1)S(1)}, u32[]{:S(2)}, u32[]{:S(2)}) collective-permute-start(bf16[256,512]{1,0:T(8,128)(2,1)S(1)} %collective-permute-done.ahead), channel_id=1, source_target_pairs={{0,2},{1,7},{2,4},{3,1},{4,6},{5,3},{6,0},{7,5},{8,10},{9,15},{10,... | collective-permute-start | bytes 786440 | tf_op jit(solution)/shard_map/ppermute | solution.py:332
  28.1 3.8 %copy-start.3 = (bf16[256,512]{1,0:T(8,128)(2,1)S(1)}, bf16[256,512]{1,0:T(8,128)(2,1)}, u32[]{:S(2)}) copy-start(bf16[256,512]{1,0:T(8,128)(2,1)} %gate.1) | copy-start | bytes 786436
  30.3 1.6 %collective-permute-start.6 = (bf16[256,512]{1,0:T(8,128)(2,1)S(1)}, bf16[256,512]{1,0:T(8,128)(2,1)S(1)}, u32[]{:S(2)}, u32[]{:S(2)}) collective-permute-start(bf16[256,512]{1,0:T(8,128)(2,1)S(1)} %collective-permute-done.5.far), channel_id=1, source_target_pairs={{0,1},{1,0},{2,3},{3,2},{4,5},{5,4},{6,7},{7,6},{8,9},{9,8},{10,11... | collective-permute-start | bytes 786440 | tf_op jit(solution)/shard_map/ppermute | solution.py:335
  30.4 11.1 %collective-permute-start.7 = (bf16[16,2,16,256]{3,2,1,0:T(8,128)(2,1)}, bf16[16,2,16,256]{3,2,1,0:T(8,128)(2,1)}, u32[]{:S(2)}, u32[]{:S(2)}) collective-permute-start(bf16[16,2,16,256]{3,2,1,0:T(8,128)(2,1)} %get-tuple-element.39), channel_id=1, source_target_pairs={{0,128},{8,136},{16,144},{24,152},{32,160},{40,168},{48,176},{56,1... | collective-permute-start | bytes 786440 | tf_op jit(solution)/shard_map/ppermute | solution.py:383
  33.4 16.5 %all-to-all-start.1 = ((bf16[32,16,256]{2,1,0:T(8,128)(2,1)}), bf16[32,16,256]{2,1,0:T(8,128)(2,1)S(1)}, u32[]{:S(2)}, u32[]{:S(2)}) async-start(bf16[32,16,256]{2,1,0:T(8,128)(2,1)} %get-tuple-element.37), calls=%async_computation.1 | async-start | bytes 524288 | tf_op jit(solution)/shard_map/all_to_all | solution.py:338
  44.6 24.3 %copy-start = (bf16[256,512]{1,0:T(8,128)(2,1)S(1)}, bf16[256,512]{1,0:T(8,128)(2,1)}, u32[]{:S(2)}) copy-start(bf16[256,512]{1,0:T(8,128)(2,1)} %key.3) | copy-start | bytes 786436
  44.6 24.3 %copy-start.1 = (bf16[256,512]{1,0:T(8,128)(2,1)S(1)}, bf16[256,512]{1,0:T(8,128)(2,1)}, u32[]{:S(2)}) copy-start(bf16[256,512]{1,0:T(8,128)(2,1)} %value.3) | copy-start | bytes 786436
  44.6 24.3 %copy-start.2 = (bf16[256,512]{1,0:T(8,128)(2,1)S(1)}, bf16[256,512]{1,0:T(8,128)(2,1)}, u32[]{:S(2)}) copy-start(bf16[256,512]{1,0:T(8,128)(2,1)} %get-tuple-element.43.mix) | copy-start | bytes 786436

commit v5 on v4

--- a/solution.py
+++ b/solution.py
@@ -349,8 +349,8 @@
 
     ahead = ring(out_grad, 1)
     pair = swap(out_grad)
-    again, pair = together((out_grad, pair))
-    behind = ring(again, -1)
+
+    behind = ring(out_grad, -1)
     sent, total = call(
         prepare_kernel,
         (shape((SIDE, 2, 2, CHANS, ROWS)), partial),
@@ -369,15 +369,16 @@
     ahead, total = together((ahead, total))
     far = ring(ahead, 1)
     ahead, behind = together((ahead, behind))
+    near, away = call(
+        pick_kernel, (shape((SIDE, 2, CHANS, ROWS)), shape((SIDE, 2, CHANS, ROWS))), near,
+        spaces="v" + "hh", scratch=[sems],
+    )
+    total, away = together((total, away))
     total, later = call(
         first_mix_kernel, (partial, shape(weights(2))),
         out_weight, total, ahead, swap(ahead), behind, swap(behind),
         spaces="hvvvvv" + "vv",
-        scratch=[pltpu.VMEM(weights(4), BF), sems], flops=7_000_000_000,
-    )
-    near, away = call(
-        pick_kernel, (shape((SIDE, 2, CHANS, ROWS)), shape((SIDE, 2, CHANS, ROWS))), near,
-        spaces="v" + "hh", scratch=[sems],
+        scratch=[pltpu.VMEM(weights(4), BF), sems], flops=1,
     )
     far, total, away = together((far, total, away))
     other = lax.ppermute(away, "ctx", [(i, (i + SIDE) % PARTS) for i in range(PARTS)])

time: 70.5 us -> 70.5 us (level)
  starting transfers between devices: 25.5 us -> 23.9 us
  waiting for transfers between devices: 14 us -> 15.6 us
    ppermute x3, starting transfers between devices: 8.09 us -> 6.5 us  [ring(): return lax.ppermute(block, 'tp', hops)]
    ppermute x3, waiting for transfers between devices: 0.97 us -> 2.39 us  [ring(): return lax.ppermute(block, 'tp', hops)]
where the time goes in v5:
time: 70.5 us; the launch traced here: 70.1 us
  starting transfers between devices  23.9 us (34%)
  blocking collectives  17.4 us (25%)
  waiting for transfers between devices  15.6 us (22%)
  Pallas kernels  12.5 us (18%)
  between operations  0.78 us (1%)
    all_to_all x1, blocking collectives, exchange(): return lax.all_to_all(block, 'ctx', split_axis=0, concat_axis=0, tiled=True)  17.4 us
    pallas_call x7, Pallas kernels, call(): pl.pallas_call(kernel, out_shape=placed, in_specs=specs[:len(args)], out_...  12.5 us
    all_to_all x1, starting transfers between devices, exchange(): return lax.all_to_all(block, 'ctx', split_axis=0, concat_axis=0, tiled=True)  8.04 us
    all_to_all x1, waiting for transfers between devices, shards(): lax.all_to_all(sent, 'ctx', split_axis=0, concat_axis=0, tiled=True, axis...  7.46 us
    all_to_all x1, starting transfers between devices, shards(): lax.all_to_all(sent, 'ctx', split_axis=0, concat_axis=0, tiled=True, axis...  7.18 us
    ppermute x3, starting transfers between devices, ring(): return lax.ppermute(block, 'tp', hops)  6.5 us
    all_to_all x1, waiting for transfers between devices, exchange(): return lax.all_to_all(block, 'ctx', split_axis=0, concat_axis=0, tiled=True)  5.26 us
    ppermute x3, waiting for transfers between devices, ring(): return lax.ppermute(block, 'tp', hops)  2.39 us
  transfers between devices with their start and end apart: 10, of which 4 were waited for; matrix products, arithmetic and copies ran while one was open for 0% of the time, Pallas kernels for 14%

profile of v5, /device:TPU:32, one launch (start us, length us, event | category | flops | bytes accessed | tf_op | source)
XLA Modules:
  0.0 70.1 jit_solution(7426419620259607416)
XLA Ops:
  0.6 0.1 collective-permute-start.1
  0.7 3.3 %collective-permute-start = (bf16[256,512]{1,0:T(8,128)(2,1)}, bf16[256,512]{1,0:T(8,128)(2,1)S(1)}, u32[]{:S(2)}, u32[]{:S(2)}) collective-permute-start(bf16[256,512]{1,0:T(8,128)(2,1)} %own.1), channel_id=1, source_target_pairs={{0,2},{1,7},{2,4},{3,1},{4,6},{5,3},{6,0},{7,5},{8,10},{9,15},{10,... | collective-permute-start | bytes 786440 | tf_op jit(solution)/shard_map/ppermute | solution.py:332
  4.1 2.2 %collective-permute-start.2 = (bf16[256,512]{1,0:T(8,128)(2,1)}, bf16[256,512]{1,0:T(8,128)(2,1)S(1)}, u32[]{:S(2)}, u32[]{:S(2)}) collective-permute-start(bf16[256,512]{1,0:T(8,128)(2,1)} %own.1), channel_id=1, source_target_pairs={{0,6},{1,3},{2,0},{3,5},{4,2},{5,7},{6,4},{7,1},{8,14},{9,11},{10,... | collective-permute-start | bytes 786440 | tf_op jit(solution)/shard_map/ppermute | solution.py:332
  6.3 0.0 collective-permute-done.1.pair
  6.3 2.2 %shard_map.111 = (bf16[16,2,2,16,256]{4,3,2,1,0:T(8,128)(2,1)}, f32[256,512]{1,0:T(8,128)S(1)}) custom-call(bf16[256,512]{1,0:T(8,128)(2,1)} %key.3, bf16[256,512]{1,0:T(8,128)(2,1)} %value.3, f32[256,512]{1,0:T(8,128)} %taps.1, bf16[256,512]{1,0:T(8,128)(2,1)} %own.1, bf16[512,4096]{1,0:T(8,128)(2,1)} %weight.3, ...), custom_call_target="tpu_custom_call" | custom-call | flops 270000000 | bytes 6815744 | tf_op jit(solution)/shard_map/pallas_call | solution.py:310
  8.5 0.0 copy-start.3
  8.5 7.2 %all-to-all-start = ((bf16[16,2,2,16,256]{4,3,2,1,0:T(8,128)(2,1)}), bf16[16,2,2,16,256]{4,3,2,1,0:T(8,128)(2,1)S(1)}, u32[]{:S(2)}, u32[]{:S(2)}) async-start(bf16[16,2,2,16,256]{4,3,2,1,0:T(8,128)(2,1)} %get-tuple-element.26), calls=%async_computation | async-start | bytes 1048576 | tf_op jit(solution)/shard_map/all_to_all | solution.py:366
  15.7 2.4 %collective-permute-done.ahead = bf16[256,512]{1,0:T(8,128)(2,1)S(1)} collective-permute-done((bf16[256,512]{1,0:T(8,128)(2,1)}, bf16[256,512]{1,0:T(8,128)(2,1)S(1)}, u32[]{:S(2)}, u32[]{:S(2)}) %collective-permute-start) | collective-permute-done | bytes 262176 | tf_op jit(solution)/shard_map/ppermute | solution.py:332
  18.1 0.0 collective-permute-done.2.behind
  18.1 0.9 %collective-permute-start.3 = (bf16[256,512]{1,0:T(8,128)(2,1)S(1)}, bf16[256,512]{1,0:T(8,128)(2,1)S(1)}, u32[]{:S(2)}, u32[]{:S(2)}) collective-permute-start(bf16[256,512]{1,0:T(8,128)(2,1)S(1)} %collective-permute-done.ahead), channel_id=1, source_target_pairs={{0,1},{1,0},{2,3},{3,2},{4,5},{5,4},{6,7},{7,6},{8,9},{9,8},{10,11... | collective-permute-start | bytes 786440 | tf_op jit(solution)/shard_map/ppermute | solution.py:335
  19.0 0.0 collective-permute-start.4
  19.0 0.9 %collective-permute-start.5 = (bf16[256,512]{1,0:T(8,128)(2,1)S(1)}, bf16[256,512]{1,0:T(8,128)(2,1)S(1)}, u32[]{:S(2)}, u32[]{:S(2)}) collective-permute-start(bf16[256,512]{1,0:T(8,128)(2,1)S(1)} %collective-permute-done.ahead), channel_id=1, source_target_pairs={{0,2},{1,7},{2,4},{3,1},{4,6},{5,3},{6,0},{7,5},{8,10},{9,15},{10,... | collective-permute-start | bytes 786440 | tf_op jit(solution)/shard_map/ppermute | solution.py:332
  20.0 7.5 %all-to-all-done.got = bf16[16,2,2,16,256]{4,3,2,1,0:T(8,128)(2,1)S(1)} async-done(((bf16[16,2,2,16,256]{4,3,2,1,0:T(8,128)(2,1)}), bf16[16,2,2,16,256]{4,3,2,1,0:T(8,128)(2,1)S(1)}, u32[]{:S(2)}, u32[]{:S(2)}) %all-to-all-start) | async-done | bytes 524320 | tf_op jit(solution)/shard_map/all_to_all | solution.py:366
  27.4 0.8 %shard_map.112 = (bf16[16,2,16,256]{3,2,1,0:T(8,128)(2,1)}, bf16[16,2,16,256]{3,2,1,0:T(8,128)(2,1)}) custom-call(bf16[16,2,2,16,256]{4,3,2,1,0:T(8,128)(2,1)S(1)} %all-to-all-done.got), custom_call_target="tpu_custom_call" | custom-call | bytes 1048576 | tf_op jit(solution)/shard_map/pallas_call | solution.py:310
  28.3 0.0 collective-permute-done.3.ahead_pair
  28.3 0.0 collective-permute-done.4.behind_pair
  28.3 2.1 %shard_map.113 = (f32[256,512]{1,0:T(8,128)S(1)}, bf16[2,512,512]{2,1,0:T(8,128)(2,1)S(1)}) custom-call(bf16[512,4096]{1,0:T(8,128)(2,1)} %weight.3, f32[256,512]{1,0:T(8,128)S(1)} %get-tuple-element.28.before, bf16[256,512]{1,0:T(8,128)(2,1)S(1)} %collective-permute-done.ahead, bf16[256,512]{1,0:T(8,128)(2,1)S(1)} %collective-permute-done.3.ahead_pair, ...), custom_call_target="tpu_custom_call" | custom-call | flops 1 | bytes 7340032 | tf_op jit(solution)/shard_map/pallas_call | solution.py:310
  30.4 0.0 collective-permute-done.5.far
  30.4 0.1 collective-permute-start.6
  30.5 1.1 %collective-permute-start.7 = (bf16[16,2,16,256]{3,2,1,0:T(8,128)(2,1)}, bf16[16,2,16,256]{3,2,1,0:T(8,128)(2,1)}, u32[]{:S(2)}, u32[]{:S(2)}) collective-permute-start(bf16[16,2,16,256]{3,2,1,0:T(8,128)(2,1)} %get-tuple-element.39), channel_id=1, source_target_pairs={{0,128},{8,136},{16,144},{24,152},{32,160},{40,168},{48,176},{56,1... | collective-permute-start | bytes 786440 | tf_op jit(solution)/shard_map/ppermute | solution.py:384
  31.6 0.4 collective-permute-done.6.far_pair
  32.1 0.0 copy-done.3
  32.1 1.4 %shard_map.114 = (bf16[256,512]{1,0:T(8,128)(2,1)}, bf16[32,16,256]{2,1,0:T(8,128)(2,1)}) custom-call(bf16[2,512,512]{2,1,0:T(8,128)(2,1)S(1)} %get-tuple-element.32.weight, f32[256,512]{1,0:T(8,128)S(1)} %get-tuple-element.35.total, bf16[256,512]{1,0:T(8,128)(2,1)S(1)} %collective-permute-done.5.far, bf16[256,512]{1,0:T(8,128)(2,1)S(1)} %collective-permute-done.6.far_pair, ...), custom_call_target="tpu_custom_call" | custom-call | flops 299999985664 | bytes 2883584 | tf_op jit(solution)/shard_map/pallas_call | solution.py:310
  33.5 8.0 %all-to-all-start.1 = ((bf16[32,16,256]{2,1,0:T(8,128)(2,1)}), bf16[32,16,256]{2,1,0:T(8,128)(2,1)S(1)}, u32[]{:S(2)}, u32[]{:S(2)}) async-start(bf16[32,16,256]{2,1,0:T(8,128)(2,1)} %get-tuple-element.37), calls=%async_computation.1 | async-start | bytes 524288 | tf_op jit(solution)/shard_map/all_to_all | solution.py:338
  41.5 0.0 collective-permute-done.7.other
  41.5 3.1 %shard_map.115 = (bf16[10,256,256]{2,1,0:T(8,128)(2,1)S(1)}, bf16[8,256,256]{2,1,0:T(8,128)(2,1)S(1)}, f32[2,32,256]{2,1,0:T(8,128)S(1)}) custom-call(bf16[16,2,16,256]{3,2,1,0:T(8,128)(2,1)} %get-tuple-element.38.near, bf16[16,2,16,256]{3,2,1,0:T(8,128)(2,1)} %collective-permute-done.7.other, bf16[1024,512]{1,0:T(8,128)(2,1)} %constant.4.clone.table, ...), custom_call_target="tpu_custom_call" | custom-call | flops 20000000000 | bytes 4063232 | tf_op jit(solution)/shard_map/pallas_call | solution.py:310
  44.6 0.0 copy-start
  44.6 0.0 copy-start.1
  44.6 0.0 copy-start.2
  44.6 5.3 %all-to-all-done.1.got = bf16[32,16,256]{2,1,0:T(8,128)(2,1)S(1)} async-done(((bf16[32,16,256]{2,1,0:T(8,128)(2,1)}), bf16[32,16,256]{2,1,0:T(8,128)(2,1)S(1)}, u32[]{:S(2)}, u32[]{:S(2)}) %all-to-all-start.1) | async-done | bytes 262176 | tf_op jit(solution)/shard_map/all_to_all | solution.py:338
  49.9 1.6 %shard_map.116 = bf16[32,3,16,256]{3,2,1,0:T(8,128)(2,1)S(1)} custom-call(bf16[32,16,256]{2,1,0:T(8,128)(2,1)S(1)} %all-to-all-done.1.got, bf16[10,256,256]{2,1,0:T(8,128)(2,1)S(1)} %get-tuple-element.40.refs_0_, bf16[8,256,256]{2,1,0:T(8,128)(2,1)S(1)} %get-tuple-element.41.refs_1_, f32[2,32,256]{2,1,0:T(8,128)S(1)} %get-tuple-element.42.refs_2_), custom_call_target="tpu_custom_call" | custom-call | flops 1200000000 | bytes 3473408 | tf_op jit(solution)/shard_map/pallas_call | solution.py:310
  51.5 17.4 %all_to_all.15.got = bf16[32,3,16,256]{3,2,1,0:T(8,128)(2,1)S(1)} all-to-all(bf16[32,3,16,256]{3,2,1,0:T(8,128)(2,1)S(1)} %shard_map.116), channel_id=1, replica_groups=mesh['ctx'=32,'tp'=8] {'ctx'}, dimensions={0} | all-to-all | bytes 1572864 | tf_op jit(solution)/shard_map/all_to_all | solution.py:338
  68.9 0.0 copy-done
  68.9 0.0 copy-done.1
  68.9 0.0 copy-done.2
  68.9 1.2 %shard_map.117 = (bf16[256,512]{1,0:T(8,128)(2,1)}, bf16[256,512]{1,0:T(8,128)(2,1)}, bf16[256,512]{1,0:T(8,128)(2,1)}, f32[256,512]{1,0:T(8,128)}) custom-call(bf16[32,3,16,256]{3,2,1,0:T(8,128)(2,1)S(1)} %all_to_all.15.got, bf16[256,512]{1,0:T(8,128)(2,1)S(1)} %copy-done.2, bf16[256,512]{1,0:T(8,128)(2,1)S(1)} %copy-done, bf16[256,512]{1,0:T(8,128)(2,1)S(1)} %copy-done.1), custom_call_target="tpu_custom_call" | custom-call | bytes 2883584 | tf_op jit(solution)/shard_map/pallas_call | solution.py:310
Async XLA Ops:
  0.6 5.7 %collective-permute-start.1 = (bf16[256,512]{1,0:T(8,128)(2,1)}, bf16[256,512]{1,0:T(8,128)(2,1)S(1)}, u32[]{:S(2)}, u32[]{:S(2)}) collective-permute-start(bf16[256,512]{1,0:T(8,128)(2,1)} %own.1), channel_id=1, source_target_pairs={{0,1},{1,0},{2,3},{3,2},{4,5},{5,4},{6,7},{7,6},{8,9},{9,8},{10,11... | collective-permute-start | bytes 786440 | tf_op jit(solution)/shard_map/ppermute | solution.py:335
  0.7 17.4 %collective-permute-start = (bf16[256,512]{1,0:T(8,128)(2,1)}, bf16[256,512]{1,0:T(8,128)(2,1)S(1)}, u32[]{:S(2)}, u32[]{:S(2)}) collective-permute-start(bf16[256,512]{1,0:T(8,128)(2,1)} %own.1), channel_id=1, source_target_pairs={{0,2},{1,7},{2,4},{3,1},{4,6},{5,3},{6,0},{7,5},{8,10},{9,15},{10,... | collective-permute-start | bytes 786440 | tf_op jit(solution)/shard_map/ppermute | solution.py:332
  4.1 14.0 %collective-permute-start.2 = (bf16[256,512]{1,0:T(8,128)(2,1)}, bf16[256,512]{1,0:T(8,128)(2,1)S(1)}, u32[]{:S(2)}, u32[]{:S(2)}) collective-permute-start(bf16[256,512]{1,0:T(8,128)(2,1)} %own.1), channel_id=1, source_target_pairs={{0,6},{1,3},{2,0},{3,5},{4,2},{5,7},{6,4},{7,1},{8,14},{9,11},{10,... | collective-permute-start | bytes 786440 | tf_op jit(solution)/shard_map/ppermute | solution.py:332
  8.5 23.6 %copy-start.3 = (bf16[256,512]{1,0:T(8,128)(2,1)S(1)}, bf16[256,512]{1,0:T(8,128)(2,1)}, u32[]{:S(2)}) copy-start(bf16[256,512]{1,0:T(8,128)(2,1)} %gate.1) | copy-start | bytes 786436
  8.5 18.9 %all-to-all-start = ((bf16[16,2,2,16,256]{4,3,2,1,0:T(8,128)(2,1)}), bf16[16,2,2,16,256]{4,3,2,1,0:T(8,128)(2,1)S(1)}, u32[]{:S(2)}, u32[]{:S(2)}) async-start(bf16[16,2,2,16,256]{4,3,2,1,0:T(8,128)(2,1)} %get-tuple-element.26), calls=%async_computation | async-start | bytes 1048576 | tf_op jit(solution)/shard_map/all_to_all | solution.py:366
  18.1 10.2 %collective-permute-start.3 = (bf16[256,512]{1,0:T(8,128)(2,1)S(1)}, bf16[256,512]{1,0:T(8,128)(2,1)S(1)}, u32[]{:S(2)}, u32[]{:S(2)}) collective-permute-start(bf16[256,512]{1,0:T(8,128)(2,1)S(1)} %collective-permute-done.ahead), channel_id=1, source_target_pairs={{0,1},{1,0},{2,3},{3,2},{4,5},{5,4},{6,7},{7,6},{8,9},{9,8},{10,11... | collective-permute-start | bytes 786440 | tf_op jit(solution)/shard_map/ppermute | solution.py:335
  19.0 9.3 %collective-permute-start.4 = (bf16[256,512]{1,0:T(8,128)(2,1)S(1)}, bf16[256,512]{1,0:T(8,128)(2,1)S(1)}, u32[]{:S(2)}, u32[]{:S(2)}) collective-permute-start(bf16[256,512]{1,0:T(8,128)(2,1)S(1)} %collective-permute-done.2.behind), channel_id=1, source_target_pairs={{0,1},{1,0},{2,3},{3,2},{4,5},{5,4},{6,7},{7,6},{8,9},{9,8},{10,11... | collective-permute-start | bytes 786440 | tf_op jit(solution)/shard_map/ppermute | solution.py:335
  19.0 11.4 %collective-permute-start.5 = (bf16[256,512]{1,0:T(8,128)(2,1)S(1)}, bf16[256,512]{1,0:T(8,128)(2,1)S(1)}, u32[]{:S(2)}, u32[]{:S(2)}) collective-permute-start(bf16[256,512]{1,0:T(8,128)(2,1)S(1)} %collective-permute-done.ahead), channel_id=1, source_target_pairs={{0,2},{1,7},{2,4},{3,1},{4,6},{5,3},{6,0},{7,5},{8,10},{9,15},{10,... | collective-permute-start | bytes 786440 | tf_op jit(solution)/shard_map/ppermute | solution.py:332
  30.4 1.6 %collective-permute-start.6 = (bf16[256,512]{1,0:T(8,128)(2,1)S(1)}, bf16[256,512]{1,0:T(8,128)(2,1)S(1)}, u32[]{:S(2)}, u32[]{:S(2)}) collective-permute-start(bf16[256,512]{1,0:T(8,128)(2,1)S(1)} %collective-permute-done.5.far), channel_id=1, source_target_pairs={{0,1},{1,0},{2,3},{3,2},{4,5},{5,4},{6,7},{7,6},{8,9},{9,8},{10,11... | collective-permute-start | bytes 786440 | tf_op jit(solution)/shard_map/ppermute | solution.py:335
  30.5 11.0 %collective-permute-start.7 = (bf16[16,2,16,256]{3,2,1,0:T(8,128)(2,1)}, bf16[16,2,16,256]{3,2,1,0:T(8,128)(2,1)}, u32[]{:S(2)}, u32[]{:S(2)}) collective-permute-start(bf16[16,2,16,256]{3,2,1,0:T(8,128)(2,1)} %get-tuple-element.39), channel_id=1, source_target_pairs={{0,128},{8,136},{16,144},{24,152},{32,160},{40,168},{48,176},{56,1... | collective-permute-start | bytes 786440 | tf_op jit(solution)/shard_map/ppermute | solution.py:384
  33.5 16.4 %all-to-all-start.1 = ((bf16[32,16,256]{2,1,0:T(8,128)(2,1)}), bf16[32,16,256]{2,1,0:T(8,128)(2,1)S(1)}, u32[]{:S(2)}, u32[]{:S(2)}) async-start(bf16[32,16,256]{2,1,0:T(8,128)(2,1)} %get-tuple-element.37), calls=%async_computation.1 | async-start | bytes 524288 | tf_op jit(solution)/shard_map/all_to_all | solution.py:338
  44.6 24.3 %copy-start = (bf16[256,512]{1,0:T(8,128)(2,1)S(1)}, bf16[256,512]{1,0:T(8,128)(2,1)}, u32[]{:S(2)}) copy-start(bf16[256,512]{1,0:T(8,128)(2,1)} %key.3) | copy-start | bytes 786436
  44.6 24.3 %copy-start.1 = (bf16[256,512]{1,0:T(8,128)(2,1)S(1)}, bf16[256,512]{1,0:T(8,128)(2,1)}, u32[]{:S(2)}) copy-start(bf16[256,512]{1,0:T(8,128)(2,1)} %value.3) | copy-start | bytes 786436
  44.6 24.3 %copy-start.2 = (bf16[256,512]{1,0:T(8,128)(2,1)S(1)}, bf16[256,512]{1,0:T(8,128)(2,1)}, u32[]{:S(2)}) copy-start(bf16[256,512]{1,0:T(8,128)(2,1)} %get-tuple-element.43.mix) | copy-start | bytes 786436
